TPU v7x, 32 devices: a whole 2x2x4 slice. The times are simulated.
32 devices in a mesh: seq: 16 (over z, y, core), samp: 2 (over x).
Axes of the slice: x: 2, y: 2, z: 4, core: 2. Of those that a mesh axis runs over, the one named last changes fastest.
Arguments:
- trunk: bfloat16 [2, 4096, 768], P('samp', 'seq'), may hold values from -6 to 6
- conv_weight: bfloat16 [3, 3, 768, 768], replicated, may hold values from -0.125 to 0.125
- head_weight: bfloat16 [768, 2688], replicated, may hold values from -0.21875 to 0.21875
- targets: int32 [2, 4096, 2688], P('samp', 'seq'), may hold values from 0 to 8
- error_mask: int32 [2, 4096], P('samp', 'seq'), may hold values 0 or 1
- upweight: int32 [2, 4096], P('samp', 'seq'), may hold values from 1 to 16, as said below
Outputs:
- loss: float32 [], replicated
- grad_conv: float32 [3, 2304, 768], P(None, 'seq', 'samp')
- grad_head: float32 [768, 2688], P('seq', 'samp')
- trunk_input_gradient: bfloat16 [2, 4096, 768], P('samp', 'seq')
Inputs may be any that keep to these rules, and one draw needn't show every extreme that they name: upweight is 1 at the first bin of each window and 16 at the last; at bin p it is at most 1 + (15 p) // 4095.
All inputs are finite; a program needn't handle non-finite values. No bound on the sum of `error_mask` on one device may be relied on, other than what follows from the above.
Results may differ from a plain program's by a relative error of at most 0.015.
Values may be sent and summed in bfloat16 or wider, within the bound.
A program may use at most 192 MiB of HBM per device.

v0:
```python
import jax
import jax.numpy as jnp
from jax import lax
from jax.sharding import PartitionSpec as P

OUTPUT_TRACKS = 2688
LAYERS = 3
BASE_DILATION = 64


def extended(shard, sides, width):
    for axis, dim in sides:
        devices, length = (lax.axis_size(axis), shard.shape[dim])
        up = [(i, (i + 1) % devices) for i in range(devices - 1)]
        down = [(j, i) for i, j in up]
        last = lax.slice_in_dim(shard, length - width, length, axis=dim)
        first = lax.slice_in_dim(shard, 0, width, axis=dim)
        before = lax.ppermute(last, axis, up)
        after = lax.ppermute(first, axis, down)
        shard = jnp.concatenate([before, shard, after], axis=dim)
    return shard


def smooth(values):
    return jax.nn.gelu(values, approximate=True)


def per_device(trunk, conv_weight, head_weight, targets, error_mask, upweight):
    windows = trunk.shape[0]
    positions = trunk.shape[1]
    channels = trunk.shape[2]
    row_count = windows * positions
    bins_all = row_count * lax.axis_size("seq") * lax.axis_size("samp")
    bin_weight = jnp.where(error_mask == 1, upweight, 1).astype(jnp.float32)
    weight_part = jnp.sum(bin_weight)
    weight_sum = lax.psum(weight_part, ("seq", "samp"))
    stream = trunk
    stored = []
    padded_acts = []
    for layer_number in range(LAYERS):
        dilation_spread = BASE_DILATION * 2**layer_number
        activated = smooth(stream.astype(jnp.float32)).astype(jnp.bfloat16)
        padded = extended(activated, (("seq", 1),), dilation_spread)
        tap_views = [
            padded[:, tap_num * dilation_spread : tap_num * dilation_spread + positions]
            for tap_num in range(3)
        ]
        conv_out = jnp.zeros((row_count, channels), jnp.float32)
        for tap_num in range(3):
            conv_out = conv_out + jnp.dot(
                tap_views[tap_num].reshape(row_count, channels),
                conv_weight[layer_number, tap_num],
                preferred_element_type=jnp.float32,
            )
        stored.append(stream)
        padded_acts.append(tap_views)
        stream = (stream.astype(jnp.float32) + conv_out.reshape(stream.shape)).astype(jnp.bfloat16)
    residual_rows = stream.reshape(row_count, channels)
    logits = jnp.dot(residual_rows, head_weight, preferred_element_type=jnp.float32)
    predicted = jax.nn.softplus(logits)
    slope = jax.nn.sigmoid(logits)
    counts = targets.reshape(row_count, -1).astype(jnp.float32)
    flat_weight = bin_weight.reshape(row_count, 1)
    partial_loss = jnp.sum(flat_weight * (predicted - counts * jnp.log(predicted)))
    loss_sum = lax.psum(partial_loss, ("seq", "samp"))
    factor = bins_all / weight_sum
    logit_grad = (factor * flat_weight * (1.0 - counts / predicted) * slope).astype(jnp.bfloat16)
    head_grad = jnp.dot(residual_rows.T, logit_grad, preferred_element_type=jnp.float32)
    stream_grad = jnp.dot(logit_grad, head_weight.T, preferred_element_type=jnp.float32).reshape(
        windows, positions, channels
    )
    kernel_grads = [None] * LAYERS
    for layer_number in reversed(range(LAYERS)):
        dilation_spread = BASE_DILATION * 2**layer_number
        grad_bf = stream_grad.astype(jnp.bfloat16)
        grad_flat = grad_bf.reshape(row_count, channels)
        padded_grad = extended(grad_bf, (("seq", 1),), dilation_spread)
        grad_views = [
            padded_grad[
                :, (2 - tap_num) * dilation_spread : (2 - tap_num) * dilation_spread + positions
            ]
            for tap_num in range(3)
        ]
        tap_views = padded_acts[layer_number]
        pieces = []
        act_grad = jnp.zeros((row_count, channels), jnp.float32)
        for tap_num in range(3):
            pieces.append(
                jnp.dot(
                    tap_views[tap_num].reshape(row_count, channels).T,
                    grad_flat,
                    preferred_element_type=jnp.float32,
                )
            )
            act_grad = act_grad + jnp.dot(
                grad_views[tap_num].reshape(row_count, channels),
                conv_weight[layer_number, tap_num].T,
                preferred_element_type=jnp.float32,
            )
        kernel_grad = jnp.concatenate(pieces, axis=0)
        kernel_grads[layer_number] = kernel_grad
        residual_float32 = stored[layer_number].astype(jnp.float32)
        pullback = jax.vjp(smooth, residual_float32)[1]
        stream_grad = stream_grad + pullback(act_grad.reshape(residual_float32.shape))[0]
    conv_share, head_share = (
        lax.psum_scatter(jnp.stack(kernel_grads, axis=0), "seq", scatter_dimension=1, tiled=True),
        lax.psum_scatter(head_grad, "seq", scatter_dimension=0, tiled=True),
    )
    conv_total, head_total = (
        lax.psum_scatter(
            conv_share.astype(jnp.bfloat16), "samp", scatter_dimension=2, tiled=True
        ).astype(jnp.float32),
        lax.psum_scatter(
            head_share.astype(jnp.bfloat16), "samp", scatter_dimension=1, tiled=True
        ).astype(jnp.float32),
    )
    loss = loss_sum / (OUTPUT_TRACKS * weight_sum)
    return (loss, conv_total, head_total, stream_grad.astype(jnp.bfloat16))


def solution(mesh):
    return jax.shard_map(
        per_device,
        mesh=mesh,
        in_specs=(
            P("samp", "seq", None),
            P(),
            P(),
            P("samp", "seq", None),
            P("samp", "seq"),
            P("samp", "seq"),
        ),
        out_specs=(P(), P(None, "seq", "samp"), P("seq", "samp"), P("samp", "seq", None)),
        check_vma=False,
    )
```

profile of v0, /device:TPU:0, one launch (start us, length us, event | category | flops | bytes accessed | tf_op | source)
XLA Modules:
  0.0 476.4 jit_solution(2349069060445583504)
XLA Ops:
  7.2 1.3 fusion.87
  8.5 2.4 collective-permute-start
  10.9 1.4 collective-permute-start.1
  12.3 2.2 fusion.49
  14.5 1.8 collective-permute-done.1
  16.3 1.8 fusion.45
  18.2 2.0 fusion.93
  20.2 5.2 %collective-permute-start.2 = (bf16[1,128,768]{2,1,0:T(8,128)(2,1)S(1)}, bf16[1,128,768]{2,1,0:T(8,128)(2,1)S(1)}, u32[]{:S(2)}, u32[]{:S(2)}) collective-permute-start(bf16[1,128,768]{2,1,0:T(8,128)(2,1)S(1)} %get-tuple-element.12), channel_id=1, source_target_pairs={{0,2},{2,4},{4,6},{6,8},{8,10},{10,12},{12,14},{14,16},{16,18},{18... | collective-permute-start | bytes 589832 | tf_op jit(solution)/shard_map/ppermute | solution.py:18
  25.4 1.3 collective-permute-start.3
  27.3 1.4 collective-permute-done.3
  30.1 1.3 collective-permute-start.5
  32.1 7.0 %collective-permute-start.4 = (bf16[1,256,768]{2,1,0:T(8,128)(2,1)S(1)}, bf16[1,256,768]{2,1,0:T(8,128)(2,1)S(1)}, u32[]{:S(2)}, u32[]{:S(2)}) collective-permute-start(bf16[1,256,768]{2,1,0:T(8,128)(2,1)S(1)} %get-tuple-element.18), channel_id=1, source_target_pairs={{0,2},{2,4},{4,6},{6,8},{8,10},{10,12},{12,14},{14,16},{16,18},{18... | collective-permute-start | bytes 1179656 | tf_op jit(solution)/shard_map/ppermute | solution.py:18
  41.2 1.2 copy-done.1
  42.4 4.8 %fusion.2 = (f32[]{:T(128)}, f32[256,2688]{1,0:T(8,128)}) fusion(s32[1,256,2688]{2,1,0:T(8,128)S(1)} %copy-done.1, f32[256]{0:T(256)S(1)} %bitcast.225, bf16[256,768]{1,0:T(8,128)(2,1)S(1)} %fusion.22, bf16[768,2688]{1,0:T(8,128)(2,1)S(1)} %copy-done.17), kind=kOutput, calls=%fused_computation.9 | convolution fusion | flops 1064534016 | bytes 10028036 | tf_op jit(solution)/shard_map/dot_general | solution.py:59
  47.2 49.5 %all-reduce = (f32[]{:T(128)}, f32[]{:T(128)}) all-reduce(f32[]{:T(128)} %get-tuple-element.20, f32[]{:T(128)} %get-tuple-element.6), channel_id=1, replica_groups=mesh['seq'=16,'samp'=2] {'seq','samp'}, use_global_device_ids=true, to_apply=%region_1.2 | all-reduce | flops 2 | bytes 16 | tf_op jit(solution)/shard_map/psum | solution.py:65
  97.5 4.2 fusion.6
  101.7 4.6 fusion.189
  106.5 3.5 fusion.186
  110.0 1.4 collective-permute-start.7
  111.5 1.3 collective-permute-start.6
  115.1 1.9 fusion.27
  117.0 1.9 fusion.23
  118.9 2.3 fusion.187
  121.3 1.3 collective-permute-start.8
  122.6 9.3 %collective-permute-start.9 = (bf16[1,128,768]{2,1,0:T(8,128)(2,1)S(1)}, bf16[1,128,768]{2,1,0:T(8,128)(2,1)S(1)}, u32[]{:S(2)}, u32[]{:S(2)}) collective-permute-start(bf16[1,128,768]{2,1,0:T(8,128)(2,1)S(1)} %get-tuple-element.11), channel_id=1, source_target_pairs={{0,2},{2,4},{4,6},{6,8},{8,10},{10,12},{12,14},{14,16},{16,18},{18... | collective-permute-start | bytes 589832 | tf_op jit(solution)/shard_map/ppermute | solution.py:18
  134.2 1.8 fusion.37
  136.0 1.8 fusion.33
  137.8 3.5 fusion.188
  143.9 7.5 %pad_maximum_fusion = f32[3,2304,768]{2,1,0:T(8,128)} fusion(f32[1,2304,768]{2,1,0:T(8,128)S(1)} %maximum_bitcast_fusion.2, f32[1,2304,768]{2,1,0:T(8,128)S(1)} %maximum_bitcast_fusion.1, f32[1,2304,768]{2,1,0:T(8,128)S(1)} %maximum_bitcast_fusion), kind=kLoop, calls=%fused_computation | loop fusion | flops 10616832 | bytes 42467328 | tf_op jit(solution)/shard_map/stack | solution.py:106
  151.4 59.3 %reduce-scatter.11.cloned.1.call-done = f32[48,2688]{1,0:T(8,128)} async-done(((f32[768,2688]{1,0:T(8,128)}), f32[48,2688]{1,0:T(8,128)}) %reduce-scatter.11.cloned.1.call-update) | async-done | bytes 516112 | tf_op jit(solution)/shard_map/reduce_scatter | solution.py:107
  210.7 1.1 convert_element_type.91
  211.8 1.2 copy.12
  213.0 214.5 %reduce-scatter.9.cloned.1.call-done = f32[3,144,768]{2,1,0:T(8,128)} async-done(((f32[3,2304,768]{2,1,0:T(8,128)}), f32[3,144,768]{2,1,0:T(8,128)}) %reduce-scatter.9.cloned.1.call-update) | async-done | bytes 1327120 | tf_op jit(solution)/shard_map/reduce_scatter | solution.py:106
  427.5 1.4 convert_element_type.89
  428.9 1.0 copy.10
  429.9 2.0 reshape.134
  433.2 1.8 collective-permute-start.11
  435.0 1.8 fusion.47
  436.7 1.5 collective-permute-start.10
  438.3 1.8 fusion.43
  440.1 1.1 collective-permute-done.10
  441.1 3.0 fusion.83
  444.1 1.2 reduce-scatter.15.cloned.1.call-done
  445.3 1.1 copy.13
  447.2 17.8 %reduce-scatter.13.cloned.1.call-done = bf16[384,432]{1,0:T(8,128)(2,1)} async-done(((bf16[768,432]{1,0:T(8,128)(2,1)}), bf16[384,432]{1,0:T(8,128)(2,1)}) %reduce-scatter.13.cloned.1.call-update) | async-done | bytes 331792
  465.0 2.0 reshape.135
  467.0 0.8 copy.11
  467.9 0.9 convert_element_type.90
  (79 shorter events, 13.2 us)
Async XLA Ops:
  7.2 203.5 %reduce-scatter.11.cloned.1.call-start = ((), (), s32[]{:S(2)}) async-start(), calls=%async_computation.5 | async-start | bytes 8773632 | tf_op jit(solution)/shard_map/reduce_scatter | solution.py:107
  8.5 9.6 %collective-permute-start = (bf16[1,64,768]{2,1,0:T(8,128)(2,1)S(1)}, bf16[1,64,768]{2,1,0:T(8,128)(2,1)S(1)}, u32[]{:S(2)}, u32[]{:S(2)}) collective-permute-start(bf16[1,64,768]{2,1,0:T(8,128)(2,1)S(1)} %get-tuple-element.14), channel_id=1, source_target_pairs={{0,2},{2,4},{4,6},{6,8},{8,10},{10,12},{12,14},{14,16},{16,18},{18... | collective-permute-start | bytes 294920 | tf_op jit(solution)/shard_map/ppermute | solution.py:18
  10.9 7.3 %copy-start.2 = (bf16[1,256,768]{2,1,0:T(8,128)(2,1)S(1)}, bf16[1,256,768]{2,1,0:T(8,128)(2,1)}, u32[]{:S(2)}) copy-start(bf16[1,256,768]{2,1,0:T(8,128)(2,1)} %param.6) | copy-start | bytes 1179652
  10.9 5.5 %collective-permute-start.1 = (bf16[1,64,768]{2,1,0:T(8,128)(2,1)S(1)}, bf16[1,64,768]{2,1,0:T(8,128)(2,1)S(1)}, u32[]{:S(2)}, u32[]{:S(2)}) collective-permute-start(bf16[1,64,768]{2,1,0:T(8,128)(2,1)S(1)} %get-tuple-element.15), channel_id=1, source_target_pairs={{2,0},{4,2},{6,4},{8,6},{10,8},{12,10},{14,12},{16,14},{18,16},{20... | collective-permute-start | bytes 294920 | tf_op jit(solution)/shard_map/ppermute | solution.py:19
  12.3 14.4 %copy-start = (bf16[3,3,768,768]{3,2,1,0:T(8,128)(2,1)S(1)}, bf16[3,3,768,768]{3,2,1,0:T(8,128)(2,1)}, u32[]{:S(2)}) copy-start(bf16[3,3,768,768]{3,2,1,0:T(8,128)(2,1)} %param.7) | copy-start | bytes 31850500
  16.3 1.8 copy-start.13
  18.2 2.1 copy-start.11
  20.2 9.2 %copy-start.7 = (bf16[1,256,768]{2,1,0:T(8,128)(2,1)}, bf16[1,256,768]{2,1,0:T(8,128)(2,1)S(1)}, u32[]{:S(2)}) copy-start(bf16[1,256,768]{2,1,0:T(8,128)(2,1)S(1)} %get-tuple-element.17) | copy-start | bytes 1179652
  20.2 9.2 %collective-permute-start.2 = (bf16[1,128,768]{2,1,0:T(8,128)(2,1)S(1)}, bf16[1,128,768]{2,1,0:T(8,128)(2,1)S(1)}, u32[]{:S(2)}, u32[]{:S(2)}) collective-permute-start(bf16[1,128,768]{2,1,0:T(8,128)(2,1)S(1)} %get-tuple-element.12), channel_id=1, source_target_pairs={{0,2},{2,4},{4,6},{6,8},{8,10},{10,12},{12,14},{14,16},{16,18},{18... | collective-permute-start | bytes 589832 | tf_op jit(solution)/shard_map/ppermute | solution.py:18
  25.4 3.3 collective-permute-start.3
  28.7 0.7 copy-start.9
  29.4 2.0 copy-start.15
  29.4 2.0 copy-start.16
  30.1 10.2 %copy-start.3 = (bf16[1,256,768]{2,1,0:T(8,128)(2,1)}, bf16[1,256,768]{2,1,0:T(8,128)(2,1)S(1)}, u32[]{:S(2)}) copy-start(bf16[1,256,768]{2,1,0:T(8,128)(2,1)S(1)} %get-tuple-element.19) | copy-start | bytes 1179652
  30.1 9.6 %collective-permute-start.5 = (bf16[1,256,768]{2,1,0:T(8,128)(2,1)S(1)}, bf16[1,256,768]{2,1,0:T(8,128)(2,1)S(1)}, u32[]{:S(2)}, u32[]{:S(2)}) collective-permute-start(bf16[1,256,768]{2,1,0:T(8,128)(2,1)S(1)} %get-tuple-element.18), channel_id=1, source_target_pairs={{2,0},{4,2},{6,4},{8,6},{10,8},{12,10},{14,12},{16,14},{18,16},{20... | collective-permute-start | bytes 1179656 | tf_op jit(solution)/shard_map/ppermute | solution.py:19
  32.1 8.3 %collective-permute-start.4 = (bf16[1,256,768]{2,1,0:T(8,128)(2,1)S(1)}, bf16[1,256,768]{2,1,0:T(8,128)(2,1)S(1)}, u32[]{:S(2)}, u32[]{:S(2)}) collective-permute-start(bf16[1,256,768]{2,1,0:T(8,128)(2,1)S(1)} %get-tuple-element.18), channel_id=1, source_target_pairs={{0,2},{2,4},{4,6},{6,8},{8,10},{10,12},{12,14},{14,16},{16,18},{18... | collective-permute-start | bytes 1179656 | tf_op jit(solution)/shard_map/ppermute | solution.py:18
  39.1 2.2 copy-start.17
  39.7 2.7 copy-start.1
  40.4 0.7 copy-start.5
  106.3 6.5 %copy-start.4 = (bf16[1,256,768]{2,1,0:T(8,128)(2,1)S(1)}, bf16[1,256,768]{2,1,0:T(8,128)(2,1)}, u32[]{:S(2)}) copy-start(bf16[1,256,768]{2,1,0:T(8,128)(2,1)} %copy-done.3) | copy-start | bytes 1179652
  106.3 321.2 %reduce-scatter.9.cloned.1.call-start = ((), (), s32[]{:S(2)}) async-start(), calls=%async_computation.4 | async-start | bytes 22560768 | tf_op jit(solution)/shard_map/reduce_scatter | solution.py:106
  110.0 4.0 copy-start.6
  110.0 7.0 %collective-permute-start.7 = (bf16[1,256,768]{2,1,0:T(8,128)(2,1)S(1)}, bf16[1,256,768]{2,1,0:T(8,128)(2,1)S(1)}, u32[]{:S(2)}, u32[]{:S(2)}) collective-permute-start(bf16[1,256,768]{2,1,0:T(8,128)(2,1)S(1)} %bitcast.219), channel_id=1, source_target_pairs={{0,2},{2,4},{4,6},{6,8},{8,10},{10,12},{12,14},{14,16},{16,18},{18... | collective-permute-start | bytes 1179656 | tf_op jit(solution)/shard_map/ppermute | solution.py:18
  111.5 7.4 %collective-permute-start.6 = (bf16[1,256,768]{2,1,0:T(8,128)(2,1)S(1)}, bf16[1,256,768]{2,1,0:T(8,128)(2,1)S(1)}, u32[]{:S(2)}, u32[]{:S(2)}) collective-permute-start(bf16[1,256,768]{2,1,0:T(8,128)(2,1)S(1)} %bitcast.220), channel_id=1, source_target_pairs={{2,0},{4,2},{6,4},{8,6},{10,8},{12,10},{14,12},{16,14},{18,16},{20... | collective-permute-start | bytes 1179656 | tf_op jit(solution)/shard_map/ppermute | solution.py:19
  118.9 13.0 %copy-start.10 = (bf16[1,128,768]{2,1,0:T(8,128)(2,1)S(1)}, bf16[1,128,768]{2,1,0:T(8,128)(2,1)}, u32[]{:S(2)}) copy-start(bf16[1,128,768]{2,1,0:T(8,128)(2,1)} %copy-done.9) | copy-start | bytes 589828
  121.3 16.5 %collective-permute-start.8 = (bf16[1,128,768]{2,1,0:T(8,128)(2,1)S(1)}, bf16[1,128,768]{2,1,0:T(8,128)(2,1)S(1)}, u32[]{:S(2)}, u32[]{:S(2)}) collective-permute-start(bf16[1,128,768]{2,1,0:T(8,128)(2,1)S(1)} %get-tuple-element.10), channel_id=1, source_target_pairs={{2,0},{4,2},{6,4},{8,6},{10,8},{12,10},{14,12},{16,14},{18,16},{20... | collective-permute-start | bytes 589832 | tf_op jit(solution)/shard_map/ppermute | solution.py:19
  122.6 10.3 %copy-start.8 = (bf16[1,256,768]{2,1,0:T(8,128)(2,1)S(1)}, bf16[1,256,768]{2,1,0:T(8,128)(2,1)}, u32[]{:S(2)}) copy-start(bf16[1,256,768]{2,1,0:T(8,128)(2,1)} %copy-done.7) | copy-start | bytes 1179652
  122.6 13.4 %collective-permute-start.9 = (bf16[1,128,768]{2,1,0:T(8,128)(2,1)S(1)}, bf16[1,128,768]{2,1,0:T(8,128)(2,1)S(1)}, u32[]{:S(2)}, u32[]{:S(2)}) collective-permute-start(bf16[1,128,768]{2,1,0:T(8,128)(2,1)S(1)} %get-tuple-element.11), channel_id=1, source_target_pairs={{0,2},{2,4},{4,6},{6,8},{8,10},{10,12},{12,14},{14,16},{16,18},{18... | collective-permute-start | bytes 589832 | tf_op jit(solution)/shard_map/ppermute | solution.py:18
  137.7 3.5 copy-start.14
  141.3 0.9 copy-start.12
  151.4 293.9 %reduce-scatter.15.cloned.1.call-start = ((), (), s32[]{:S(2)}) async-start(), calls=%async_computation.7 | async-start | bytes 1032192
  213.0 252.0 %reduce-scatter.13.cloned.1.call-start = ((), (), s32[]{:S(2)}) async-start(), calls=%async_computation.6 | async-start | bytes 1179648
  431.9 9.3 %copy-start.18 = (f32[1,256,768]{2,1,0:T(8,128)S(1)}, f32[1,256,768]{2,1,0:T(8,128)}, u32[]{:S(2)}) copy-start(f32[1,256,768]{2,1,0:T(8,128)} %get-tuple-element.27) | copy-start | bytes 2359300
  433.2 5.1 %collective-permute-start.11 = (bf16[1,64,768]{2,1,0:T(8,128)(2,1)S(1)}, bf16[1,64,768]{2,1,0:T(8,128)(2,1)S(1)}, u32[]{:S(2)}, u32[]{:S(2)}) collective-permute-start(bf16[1,64,768]{2,1,0:T(8,128)(2,1)S(1)} %get-tuple-element.9), channel_id=1, source_target_pairs={{0,2},{2,4},{4,6},{6,8},{8,10},{10,12},{12,14},{14,16},{16,18},{18... | collective-permute-start | bytes 294920 | tf_op jit(solution)/shard_map/ppermute | solution.py:18
  436.7 4.4 collective-permute-start.10
Sparse Core Ops, SparseCore 0:
  106.4 104.2 reduce-scatter.10
  214.8 212.6 reduce-scatter.8
  429.9 15.4 reduce-scatter.14
  447.5 17.4 reduce-scatter.12
where the time goes:
time: 478 us; the launch traced here: 476 us
  waiting for transfers between devices  297 us (62%)
  blocking collectives  49.5 us (10%)
  matrix products  47.2 us (10%)
  starting transfers between devices  35.4 us (7%)
  other arithmetic  19.1 us (4%)
  between operations  17.5 us (4%)
  local copies, waits for them, and re-layouts  10.4 us (2%)
    reduce_scatter x1, waiting for transfers between devices, per_device(): lax.psum_scatter(jnp.stack(kernel_grads, axis=0), 'seq', scatter_dimensio...  214 us
    reduce_scatter x1, waiting for transfers between devices, per_device(): lax.psum_scatter(head_grad, 'seq', scatter_dimension=0, tiled=True)  59.3 us
    psum x1, blocking collectives, per_device(): loss_sum = lax.psum(partial_loss, ('seq', 'samp'))  49.5 us
    ppermute x6, starting transfers between devices, extended(): before = lax.ppermute(last, axis, up)  27 us
    dot_general x9, matrix products, per_device(): jnp.dot(grad_views[tap_num].reshape(row_count, channels), conv_weight[lay...  19.7 us
    unnamed x6, waiting for transfers between devices  19.1 us
    unnamed x44, local copies, waits for them, and re-layouts  10.3 us
  transfers between devices with their start and end apart: 16, of which 8 were waited for; matrix products, arithmetic and copies ran while one was open for 11% of the time, Pallas kernels for 0%

commit v1 on v0

v1 whole, which is shorter than its diff:
```python
import jax
import jax.numpy as jnp
from jax import lax
from jax.sharding import PartitionSpec as P

OUTPUT_TRACKS = 2688
LAYERS = 3
BASE_DILATION = 64


def extended(shard, width):
    devices, length = (lax.axis_size("seq"), shard.shape[1])
    up = [(i, (i + 1) % devices) for i in range(devices - 1)]
    down = [(j, i) for i, j in up]
    before = lax.ppermute(lax.slice_in_dim(shard, length - width, length, axis=1), "seq", up)
    after = lax.ppermute(lax.slice_in_dim(shard, 0, width, axis=1), "seq", down)
    return jnp.concatenate([before, shard, after], axis=1)


def smooth(values):
    return jax.nn.gelu(values, approximate=True)


def halve(part, dim, axis, bit):
    place = lax.axis_index(axis)
    mine = lax.rem(lax.div(place, 2**bit), 2)
    pairs = [(i, i ^ (2**bit)) for i in range(lax.axis_size(axis))]
    away = lax.dynamic_index_in_dim(part, 1 - mine, dim, keepdims=False)
    kept = lax.dynamic_index_in_dim(part, mine, dim, keepdims=False)
    come = lax.ppermute(away, axis, pairs)
    return (kept.astype(jnp.float32) + come.astype(jnp.float32)).astype(jnp.bfloat16)


def scatter_sum(part, order):
    labels = ["samp"] + list(reversed(range(part.ndim - 3)))
    for step in order:
        dim = labels.index(step)
        part = halve(part, dim, *(("samp", 0) if step == "samp" else ("seq", step)))
        labels.pop(dim)
    return part


def reduced(halves):
    devices = lax.axis_size("seq")
    bits = devices.bit_length() - 1
    rows = halves[0].shape[0] // devices
    stacked = jnp.stack([h.reshape((2,) * bits + (rows, h.shape[1])) for h in halves], axis=0)
    cut = max((rows * 5 // 9) // 16 * 16, 1)
    higher = list(range(2, bits))
    first = scatter_sum(stacked[..., :cut, :], [0, "samp", 1] + higher)
    second = scatter_sum(stacked[..., cut:, :], [0, 1, "samp"] + higher)
    return jnp.concatenate([first, second], axis=0).astype(jnp.float32)


def per_device(trunk, conv_weight, head_weight, targets, error_mask, upweight):
    windows, positions, channels = trunk.shape
    row_count = windows * positions
    bins_all = row_count * lax.axis_size("seq") * lax.axis_size("samp")
    bin_weight = jnp.where(error_mask == 1, upweight, 1).astype(jnp.float32)
    weight_sum = lax.psum(jnp.sum(bin_weight), ("seq", "samp"))
    stream = trunk
    stored = []
    padded_acts = []
    for layer_number in range(LAYERS):
        spread = BASE_DILATION * 2**layer_number
        activated = smooth(stream.astype(jnp.float32)).astype(jnp.bfloat16)
        padded = extended(activated, spread)
        taps = jnp.concatenate(
            [padded[:, k * spread : k * spread + positions] for k in range(3)], axis=2
        ).reshape(row_count, 3 * channels)
        conv_out = jnp.dot(
            taps,
            conv_weight[layer_number].reshape(3 * channels, channels),
            preferred_element_type=jnp.float32,
        )
        stored.append(stream)
        padded_acts.append(taps)
        stream = (stream.astype(jnp.float32) + conv_out.reshape(stream.shape)).astype(jnp.bfloat16)
    residual_rows = stream.reshape(row_count, channels)
    logits = jnp.dot(residual_rows, head_weight, preferred_element_type=jnp.float32)
    predicted = jax.nn.softplus(logits)
    slope = jax.nn.sigmoid(logits)
    counts = targets.reshape(row_count, -1).astype(jnp.float32)
    flat_weight = bin_weight.reshape(row_count, 1)
    partial_loss = jnp.sum(flat_weight * (predicted - counts * jnp.log(predicted)))
    loss_sum = lax.psum(partial_loss, ("seq", "samp"))
    factor = bins_all / weight_sum
    logit_grad = (factor * flat_weight * (1.0 - counts / predicted) * slope).astype(jnp.bfloat16)
    half = logit_grad.shape[1] // 2
    head_total = reduced(
        [
            jnp.dot(residual_rows.T, part, preferred_element_type=jnp.float32).astype(jnp.bfloat16)
            for part in (logit_grad[:, :half], logit_grad[:, half:])
        ]
    )
    stream_grad = jnp.dot(logit_grad, head_weight.T, preferred_element_type=jnp.float32).reshape(
        windows, positions, channels
    )
    kernel_grads = [None] * LAYERS
    for layer_number in reversed(range(LAYERS)):
        spread = BASE_DILATION * 2**layer_number
        grad_bf = stream_grad.astype(jnp.bfloat16)
        grad_flat = grad_bf.reshape(row_count, channels)
        padded_grad = extended(grad_bf, spread)
        side = channels // 2
        kernel_grads[layer_number] = reduced(
            [
                jnp.dot(
                    padded_acts[layer_number].T, part, preferred_element_type=jnp.float32
                ).astype(jnp.bfloat16)
                for part in (grad_flat[:, :side], grad_flat[:, side:])
            ]
        )
        act_grad = jnp.zeros((row_count, channels), jnp.float32)
        for k in range(3):
            view = padded_grad[:, (2 - k) * spread : (2 - k) * spread + positions]
            act_grad = act_grad + jnp.dot(
                view.reshape(row_count, channels),
                conv_weight[layer_number, k].T,
                preferred_element_type=jnp.float32,
            )
        residual_float32 = stored[layer_number].astype(jnp.float32)
        pullback = jax.vjp(smooth, residual_float32)[1]
        stream_grad = stream_grad + pullback(act_grad.reshape(residual_float32.shape))[0]
    loss = loss_sum / (OUTPUT_TRACKS * weight_sum)
    return (loss, jnp.stack(kernel_grads), head_total, stream_grad.astype(jnp.bfloat16))


def solution(mesh):
    return jax.shard_map(
        per_device,
        mesh=mesh,
        in_specs=(
            P("samp", "seq", None),
            P(),
            P(),
            P("samp", "seq", None),
            P("samp", "seq"),
            P("samp", "seq"),
        ),
        out_specs=(P(), P(None, "seq", "samp"), P("seq", "samp"), P("samp", "seq", None)),
        check_vma=False,
    )
```

time: 478 us -> 315 us (0.66)
  waiting for transfers between devices: 297 us -> 101 us
  starting transfers between devices: 35.4 us -> 83.9 us
  between operations: 17.5 us -> 5.07 us
  matrix products: 47.2 us -> 36.6 us
  local copies, waits for them, and re-layouts: 10.4 us -> 19.7 us
    reduce_scatter x2 -> x0, waiting for transfers between devices: 274 us -> none  [the longest x1 214 us: per_device(): lax.psum_scatter(jnp.stack(kernel_grads, axis=0), 'seq', scatter_dimensio...]
    ppermute x12 -> x52, waiting for transfers between devices: 4.46 us -> 101 us  [the longest x40 89.8 us: halve(): come = lax.ppermute(away, axis, pairs)]
    ppermute x12 -> x52, starting transfers between devices: 35.1 us -> 83.9 us  [the longest x40 54.9 us: halve(): come = lax.ppermute(away, axis, pairs)]
    unnamed x6 -> x0, waiting for transfers between devices: 19.1 us -> none
    dot_general x28 -> x20, matrix products: 38.9 us -> 29.5 us  [the longest x9 11.7 us: per_device(): jnp.dot(view.reshape(row_count, channels), conv_weight[layer_number, k].T...]
    convert_element_type x0 -> x2, local copies, waits for them, and re-layouts: none -> 7.03 us  [per_device(): jnp.dot(residual_rows.T, part, preferred_element_type=jnp.float32)]
    another operation x4 -> x6, other arithmetic: 8.97 us -> 3.15 us  [the longest x5 2.27 us: reduced(): jnp.stack([h.reshape((2,) * bits + (rows, h.shape[1])) for h in halves],...]
    unnamed x44 -> x75, local copies, waits for them, and re-layouts: 10.3 us -> 6.5 us
  transfers between devices with their start and end apart: 16 -> 52, of which waited for: 8 -> 26; matrix products, arithmetic and copies ran while one was open for 11% -> 17% of each run, Pallas kernels for 0% -> 0%
where the time goes in v1:
time: 315 us; the launch traced here: 314 us
  waiting for transfers between devices  101 us (32%)
  starting transfers between devices  83.9 us (27%)
  blocking collectives  47.2 us (15%)
  matrix products  36.6 us (12%)
  other arithmetic  20.9 us (7%)
  local copies, waits for them, and re-layouts  19.7 us (6%)
  between operations  5.07 us (2%)
    ppermute x40, waiting for transfers between devices, halve(): come = lax.ppermute(away, axis, pairs)  89.8 us
    ppermute x40, starting transfers between devices, halve(): come = lax.ppermute(away, axis, pairs)  54.9 us
    psum x1, blocking collectives, per_device(): loss_sum = lax.psum(partial_loss, ('seq', 'samp'))  47.2 us
    ppermute x6, starting transfers between devices, extended(): lax.ppermute(lax.slice_in_dim(shard, length - width, length, axis=1), 'se...  20.6 us
    dot_general x9, matrix products, per_device(): jnp.dot(view.reshape(row_count, channels), conv_weight[layer_number, k].T...  11.7 us
    ppermute x6, waiting for transfers between devices, extended(): after = lax.ppermute(lax.slice_in_dim(shard, 0, width, axis=1), 'seq', down)  11.2 us
    ppermute x6, starting transfers between devices, extended(): after = lax.ppermute(lax.slice_in_dim(shard, 0, width, axis=1), 'seq', down)  8.39 us
    convert_element_type x34, other arithmetic, halve(): (kept.astype(jnp.float32) + come.astype(jnp.float32)).astype(jnp.bfloat16)  7.54 us
  transfers between devices with their start and end apart: 52, of which 26 were waited for; matrix products, arithmetic and copies ran while one was open for 17% of the time, Pallas kernels for 0%

profile of v1, /device:TPU:0, one launch (start us, length us, event | category | flops | bytes accessed | tf_op | source)
XLA Modules:
  0.0 314.4 jit_solution(18221244092580666204)
XLA Ops:
  1.9 2.4 collective-permute-start
  5.8 4.5 %fusion.182 = (bf16[1,3,768,768]{3,2,1,0:T(8,128)(2,1)S(1)}, bf16[1,3,768,768]{3,2,1,0:T(8,128)(2,1)S(1)}, bf16[1,3,768,768]{3,2,1,0:T(8,128)(2,1)S(1)}) fusion(bf16[3,3,768,768]{3,2,1,0:T(8,128)(2,1)} %param.7), kind=kLoop, calls=%fused_computation.331 | loop fusion | bytes 21233664 | tf_op jit(solution)/shard_map/slice | solution.py:73
  11.7 5.2 %collective-permute-start.2 = (bf16[1,128,768]{2,1,0:T(8,128)(2,1)S(1)}, bf16[1,128,768]{2,1,0:T(8,128)(2,1)S(1)}, u32[]{:S(2)}, u32[]{:S(2)}) collective-permute-start(bf16[1,128,768]{2,1,0:T(8,128)(2,1)S(1)} %get-tuple-element.29), channel_id=1, source_target_pairs={{0,2},{2,4},{4,6},{6,8},{8,10},{10,12},{12,14},{14,16},{16,18},{18... | collective-permute-start | bytes 589832 | tf_op jit(solution)/shard_map/ppermute | solution.py:15
  18.2 3.2 %collective-permute-done.3 = bf16[1,128,768]{2,1,0:T(8,128)(2,1)S(1)} collective-permute-done((bf16[1,128,768]{2,1,0:T(8,128)(2,1)S(1)}, bf16[1,128,768]{2,1,0:T(8,128)(2,1)S(1)}, u32[]{:S(2)}, u32[]{:S(2)}) %collective-permute-start.3) | collective-permute-done | bytes 196640 | tf_op jit(solution)/shard_map/ppermute | solution.py:16
  21.4 2.1 fusion.100
  23.5 6.8 %collective-permute-start.4 = (bf16[1,256,768]{2,1,0:T(8,128)(2,1)}, bf16[1,256,768]{2,1,0:T(8,128)(2,1)}, u32[]{:S(2)}, u32[]{:S(2)}) collective-permute-start(bf16[1,256,768]{2,1,0:T(8,128)(2,1)} %get-tuple-element.35), channel_id=1, source_target_pairs={{0,2},{2,4},{4,6},{6,8},{8,10},{10,12},{12,14},{14,16},{16,18},{18... | collective-permute-start | bytes 1179656 | tf_op jit(solution)/shard_map/ppermute | solution.py:15
  32.3 2.0 collective-permute-done.5
  34.3 2.6 fusion.32
  37.8 4.8 %fusion.3 = (f32[]{:T(128)}, f32[256,2688]{1,0:T(8,128)}) fusion(s32[1,256,2688]{2,1,0:T(8,128)S(1)} %copy-done.4, f32[256]{0:T(256)S(1)} %bitcast.429, bf16[256,768]{1,0:T(8,128)(2,1)S(1)} %fusion.32, bf16[768,2688]{1,0:T(8,128)(2,1)S(1)} %copy-done.17), kind=kOutput, calls=%fused_computation.25 | convolution fusion | flops 1064534016 | bytes 10028036 | tf_op jit(solution)/shard_map/dot_general | solution.py:80
  42.6 47.2 %all-reduce = (f32[]{:T(128)}, f32[]{:T(128)}) all-reduce(f32[]{:T(128)} %get-tuple-element.37, f32[]{:T(128)} %get-tuple-element.6), channel_id=1, replica_groups=mesh['seq'=16,'samp'=2] {'seq','samp'}, use_global_device_ids=true, to_apply=%region_1.2 | all-reduce | flops 2 | bytes 16 | tf_op jit(solution)/shard_map/psum | solution.py:86
  90.5 3.9 %fusion.7 = bf16[256,2688]{1,0:T(8,128)(2,1)S(1)} fusion(f32[256,2688]{1,0:T(8,128)} %get-tuple-element.38, s32[1,256,2688]{2,1,0:T(8,128)S(1)} %copy-done.5, f32[256]{0:T(256)S(1)} %broadcast_multiply_fusion), kind=kLoop, calls=%fused_computation.29 | loop fusion | flops 10321920 | bytes 6882304 | tf_op jit(solution)/shard_map/convert_element_type | solution.py:88
  94.5 2.3 fusion.187
  96.8 2.0 collective-permute-start.7
  100.3 2.0 convolution_convert_fusion.7
  102.3 2.5 convolution_convert_fusion.6
  104.9 2.9 copy.24
  107.8 4.1 %copy.25 = bf16[768,1344]{1,0:T(8,128)(2,1)} copy(bf16[768,1344]{0,1:T(8,128)(2,1)} %convolution_convert_fusion.6) | data formatting | bytes 4128768 | tf_op jit(solution)/shard_map/convert_element_type | solution.py:92
  111.9 2.6 fusion.18
  116.4 3.0 collective-permute-start.40
  119.4 2.0 convolution_convert_fusion
  121.5 2.0 convolution_convert_fusion.1
  125.5 2.7 fusion.51
  131.7 2.0 fusion.49
  133.8 2.4 fusion.188
  136.2 2.3 collective-permute-start.9
  145.3 2.6 collective-permute-done.8
  147.9 4.2 %collective-permute-start.20 = (bf16[2,2,2,2,80,384]{5,4,1,2,0,3:T(8,128)(2,1)S(1)}, bf16[2,2,2,2,80,384]{5,4,1,2,0,3:T(8,128)(2,1)S(1)}, u32[]{:S(2)}, u32[]{:S(2)}) collective-permute-start(bf16[2,2,2,2,80,384]{5,4,1,2,0,3:T(8,128)(2,1)S(1)} %bitcast.421), channel_id=1, source_target_pairs={{0,2},{2,0},{4,6},{6,4},{8,10},{10,8},{12,14},{14,12},{16,18},{18,... | collective-permute-start | bytes 2949128 | tf_op jit(solution)/shard_map/ppermute | solution.py:30
  156.6 1.9 collective-permute-start.51
  161.8 3.4 %collective-permute-done.50 = bf16[1,64,768]{2,1,0:T(8,128)(2,1)S(1)} collective-permute-done((bf16[1,64,768]{2,1,0:T(8,128)(2,1)S(1)}, bf16[1,64,768]{2,1,0:T(8,128)(2,1)S(1)}, u32[]{:S(2)}, u32[]{:S(2)}) %collective-permute-start.50) | collective-permute-done | bytes 98336 | tf_op jit(solution)/shard_map/ppermute | solution.py:16
  165.2 3.9 %collective-permute-start.10 = (bf16[2,2,2,2,80,384]{5,4,1,2,0,3:T(8,128)(2,1)S(1)}, bf16[2,2,2,2,80,384]{5,4,1,2,0,3:T(8,128)(2,1)S(1)}, u32[]{:S(2)}, u32[]{:S(2)}) collective-permute-start(bf16[2,2,2,2,80,384]{5,4,1,2,0,3:T(8,128)(2,1)S(1)} %bitcast.420), channel_id=1, source_target_pairs={{0,2},{2,0},{4,6},{6,4},{8,10},{10,8},{12,14},{14,12},{16,18},{18,... | collective-permute-start | bytes 2949128 | tf_op jit(solution)/shard_map/ppermute | solution.py:30
  170.8 2.3 collective-permute-start.41
  173.4 8.3 %collective-permute-done.41 = bf16[2,2,2,16,1344]{4,3,0,1,2:T(8,128)(2,1)S(1)} collective-permute-done((bf16[2,2,2,16,1344]{4,3,0,1,2:T(8,128)(2,1)S(1)}, bf16[2,2,2,16,1344]{4,3,0,1,2:T(8,128)(2,1)S(1)}, u32[]{:S(2)}, u32[]{:S(2)}) %collective-permute-start.41) | collective-permute-done | bytes 344096 | tf_op jit(solution)/shard_map/ppermute | solution.py:30
  184.5 4.4 %collective-permute-done.42 = bf16[2,2,16,1344]{3,2,0,1:T(8,128)(2,1)S(1)} collective-permute-done((bf16[2,2,16,1344]{3,2,0,1:T(8,128)(2,1)S(1)}, bf16[2,2,16,1344]{3,2,0,1:T(8,128)(2,1)S(1)}, u32[]{:S(2)}, u32[]{:S(2)}) %collective-permute-start.42) | collective-permute-done | bytes 172064 | tf_op jit(solution)/shard_map/ppermute | solution.py:30
  190.0 9.6 %collective-permute-done.36 = bf16[2,2,2,64,384]{4,3,1,2,0:T(8,128)(2,1)S(1)} collective-permute-done((bf16[2,2,2,64,384]{4,3,1,2,0:T(8,128)(2,1)S(1)}, bf16[2,2,2,64,384]{4,3,1,2,0:T(8,128)(2,1)S(1)}, u32[]{:S(2)}, u32[]{:S(2)}) %collective-permute-start.36) | collective-permute-done | bytes 393248 | tf_op jit(solution)/shard_map/ppermute | solution.py:30
  201.1 3.0 collective-permute-done.43
  205.5 3.7 %collective-permute-done.44 = bf16[16,1344]{1,0:T(8,128)(2,1)S(1)} collective-permute-done((bf16[16,1344]{1,0:T(8,128)(2,1)S(1)}, bf16[16,1344]{1,0:T(8,128)(2,1)S(1)}, u32[]{:S(2)}, u32[]{:S(2)}) %collective-permute-start.44) | collective-permute-done | bytes 43040 | tf_op jit(solution)/shard_map/ppermute | solution.py:30
  217.8 9.3 %collective-permute-done.37 = bf16[2,2,64,384]{3,2,0,1:T(8,128)(2,1)S(1)} collective-permute-done((bf16[2,2,64,384]{3,2,0,1:T(8,128)(2,1)S(1)}, bf16[2,2,64,384]{3,2,0,1:T(8,128)(2,1)S(1)}, u32[]{:S(2)}, u32[]{:S(2)}) %collective-permute-start.37) | collective-permute-done | bytes 196640 | tf_op jit(solution)/shard_map/ppermute | solution.py:30
  229.9 3.1 collective-permute-done.38
  234.4 3.7 %collective-permute-done.39 = bf16[64,384]{1,0:T(8,128)(2,1)S(1)} collective-permute-done((bf16[64,384]{1,0:T(8,128)(2,1)S(1)}, bf16[64,384]{1,0:T(8,128)(2,1)S(1)}, u32[]{:S(2)}, u32[]{:S(2)}) %collective-permute-start.39) | collective-permute-done | bytes 49184 | tf_op jit(solution)/shard_map/ppermute | solution.py:30
  241.2 12.4 %collective-permute-done.32 = bf16[2,2,80,384]{3,2,0,1:T(8,128)(2,1)S(1)} collective-permute-done((bf16[2,2,80,384]{3,2,0,1:T(8,128)(2,1)S(1)}, bf16[2,2,80,384]{3,2,0,1:T(8,128)(2,1)S(1)}, u32[]{:S(2)}, u32[]{:S(2)}) %collective-permute-start.32) | collective-permute-done | bytes 245792 | tf_op jit(solution)/shard_map/ppermute | solution.py:30
  262.3 3.7 %collective-permute-done.34 = bf16[80,384]{1,0:T(8,128)(2,1)S(1)} collective-permute-done((bf16[80,384]{1,0:T(8,128)(2,1)S(1)}, bf16[80,384]{1,0:T(8,128)(2,1)S(1)}, u32[]{:S(2)}, u32[]{:S(2)}) %collective-permute-start.34) | collective-permute-done | bytes 61472 | tf_op jit(solution)/shard_map/ppermute | solution.py:30
  266.8 5.2 %collective-permute-done.17 = bf16[2,2,64,384]{3,2,0,1:T(8,128)(2,1)S(1)} collective-permute-done((bf16[2,2,64,384]{3,2,0,1:T(8,128)(2,1)S(1)}, bf16[2,2,64,384]{3,2,0,1:T(8,128)(2,1)S(1)}, u32[]{:S(2)}, u32[]{:S(2)}) %collective-permute-start.17) | collective-permute-done | bytes 196640 | tf_op jit(solution)/shard_map/ppermute | solution.py:30
  282.7 3.5 %collective-permute-done.23 = bf16[2,80,384]{2,1,0:T(8,128)(2,1)S(1)} collective-permute-done((bf16[2,80,384]{2,1,0:T(8,128)(2,1)S(1)}, bf16[2,80,384]{2,1,0:T(8,128)(2,1)S(1)}, u32[]{:S(2)}, u32[]{:S(2)}) %collective-permute-start.23) | collective-permute-done | bytes 122912 | tf_op jit(solution)/shard_map/ppermute | solution.py:30
  286.3 2.0 collective-permute-start.24
  288.3 3.2 %collective-permute-done.24 = bf16[80,384]{1,0:T(8,128)(2,1)S(1)} collective-permute-done((bf16[80,384]{1,0:T(8,128)(2,1)S(1)}, bf16[80,384]{1,0:T(8,128)(2,1)S(1)}, u32[]{:S(2)}, u32[]{:S(2)}) %collective-permute-start.24) | collective-permute-done | bytes 61472 | tf_op jit(solution)/shard_map/ppermute | solution.py:30
  293.5 4.6 %collective-permute-done.13 = bf16[2,80,384]{2,1,0:T(8,128)(2,1)S(1)} collective-permute-done((bf16[2,80,384]{2,1,0:T(8,128)(2,1)S(1)}, bf16[2,80,384]{2,1,0:T(8,128)(2,1)S(1)}, u32[]{:S(2)}, u32[]{:S(2)}) %collective-permute-start.13) | collective-permute-done | bytes 122912 | tf_op jit(solution)/shard_map/ppermute | solution.py:30
  301.4 4.1 %collective-permute-done.14 = bf16[80,384]{1,0:T(8,128)(2,1)S(1)} collective-permute-done((bf16[80,384]{1,0:T(8,128)(2,1)S(1)}, bf16[80,384]{1,0:T(8,128)(2,1)S(1)}, u32[]{:S(2)}, u32[]{:S(2)}) %collective-permute-start.14) | collective-permute-done | bytes 61472 | tf_op jit(solution)/shard_map/ppermute | solution.py:30
  308.2 4.3 %collective-permute-done.49 = bf16[32,1344]{1,0:T(8,128)(2,1)S(1)} collective-permute-done((bf16[32,1344]{1,0:T(8,128)(2,1)S(1)}, bf16[32,1344]{1,0:T(8,128)(2,1)S(1)}, u32[]{:S(2)}, u32[]{:S(2)}) %collective-permute-start.49) | collective-permute-done | bytes 86048 | tf_op jit(solution)/shard_map/ppermute | solution.py:30
  (250 shorter events, 83.5 us)
Async XLA Ops:
  1.9 8.3 %collective-permute-start = (bf16[1,64,768]{2,1,0:T(8,128)(2,1)S(1)}, bf16[1,64,768]{2,1,0:T(8,128)(2,1)S(1)}, u32[]{:S(2)}, u32[]{:S(2)}) collective-permute-start(bf16[1,64,768]{2,1,0:T(8,128)(2,1)S(1)} %get-tuple-element.31), channel_id=1, source_target_pairs={{0,2},{2,4},{4,6},{6,8},{8,10},{10,12},{12,14},{14,16},{16,18},{18... | collective-permute-start | bytes 294920 | tf_op jit(solution)/shard_map/ppermute | solution.py:15
  4.3 6.0 %collective-permute-start.1 = (bf16[1,64,768]{2,1,0:T(8,128)(2,1)S(1)}, bf16[1,64,768]{2,1,0:T(8,128)(2,1)S(1)}, u32[]{:S(2)}, u32[]{:S(2)}) collective-permute-start(bf16[1,64,768]{2,1,0:T(8,128)(2,1)S(1)} %get-tuple-element.32), channel_id=1, source_target_pairs={{2,0},{4,2},{6,4},{8,6},{10,8},{12,10},{14,12},{16,14},{18,16},{20... | collective-permute-start | bytes 294920 | tf_op jit(solution)/shard_map/ppermute | solution.py:16
  11.7 6.5 %collective-permute-start.2 = (bf16[1,128,768]{2,1,0:T(8,128)(2,1)S(1)}, bf16[1,128,768]{2,1,0:T(8,128)(2,1)S(1)}, u32[]{:S(2)}, u32[]{:S(2)}) collective-permute-start(bf16[1,128,768]{2,1,0:T(8,128)(2,1)S(1)} %get-tuple-element.29), channel_id=1, source_target_pairs={{0,2},{2,4},{4,6},{6,8},{8,10},{10,12},{12,14},{14,16},{16,18},{18... | collective-permute-start | bytes 589832 | tf_op jit(solution)/shard_map/ppermute | solution.py:15
  16.8 4.6 %collective-permute-start.3 = (bf16[1,128,768]{2,1,0:T(8,128)(2,1)S(1)}, bf16[1,128,768]{2,1,0:T(8,128)(2,1)S(1)}, u32[]{:S(2)}, u32[]{:S(2)}) collective-permute-start(bf16[1,128,768]{2,1,0:T(8,128)(2,1)S(1)} %get-tuple-element.30), channel_id=1, source_target_pairs={{2,0},{4,2},{6,4},{8,6},{10,8},{12,10},{14,12},{16,14},{18,16},{20... | collective-permute-start | bytes 589832 | tf_op jit(solution)/shard_map/ppermute | solution.py:16
  23.5 8.8 %collective-permute-start.4 = (bf16[1,256,768]{2,1,0:T(8,128)(2,1)}, bf16[1,256,768]{2,1,0:T(8,128)(2,1)}, u32[]{:S(2)}, u32[]{:S(2)}) collective-permute-start(bf16[1,256,768]{2,1,0:T(8,128)(2,1)} %get-tuple-element.35), channel_id=1, source_target_pairs={{0,2},{2,4},{4,6},{6,8},{8,10},{10,12},{12,14},{14,16},{16,18},{18... | collective-permute-start | bytes 1179656 | tf_op jit(solution)/shard_map/ppermute | solution.py:15
  96.8 34.8 %collective-permute-start.7 = (bf16[1,256,768]{2,1,0:T(8,128)(2,1)S(1)}, bf16[1,256,768]{2,1,0:T(8,128)(2,1)}, u32[]{:S(2)}, u32[]{:S(2)}) collective-permute-start(bf16[1,256,768]{2,1,0:T(8,128)(2,1)S(1)} %bitcast.427), channel_id=1, source_target_pairs={{0,2},{2,4},{4,6},{6,8},{8,10},{10,12},{12,14},{14,16},{16,18},{18... | collective-permute-start | bytes 1179656 | tf_op jit(solution)/shard_map/ppermute | solution.py:15
  98.8 34.9 %collective-permute-start.6 = (bf16[1,256,768]{2,1,0:T(8,128)(2,1)S(1)}, bf16[1,256,768]{2,1,0:T(8,128)(2,1)}, u32[]{:S(2)}, u32[]{:S(2)}) collective-permute-start(bf16[1,256,768]{2,1,0:T(8,128)(2,1)S(1)} %bitcast.428), channel_id=1, source_target_pairs={{2,0},{4,2},{6,4},{8,6},{10,8},{12,10},{14,12},{16,14},{18,16},{20... | collective-permute-start | bytes 1179656 | tf_op jit(solution)/shard_map/ppermute | solution.py:16
  116.4 40.2 %collective-permute-start.40 = (bf16[2,2,2,2,16,1344]{5,4,1,2,3,0:T(8,128)(2,1)}, bf16[2,2,2,2,16,1344]{5,4,1,2,3,0:T(8,128)(2,1)}, u32[]{:S(2)}, u32[]{:S(2)}) collective-permute-start(bf16[2,2,2,2,16,1344]{5,4,1,2,3,0:T(8,128)(2,1)} %bitcast.394), channel_id=1, source_target_pairs={{0,2},{2,0},{4,6},{6,4},{8,10},{10,8},{12,14},{14,12},{16,18},{18,... | collective-permute-start | bytes 2064392 | tf_op jit(solution)/shard_map/ppermute | solution.py:30
  119.4 94.1 %collective-permute-start.45 = (bf16[2,2,2,2,32,1344]{5,4,3,2,1,0:T(8,128)(2,1)}, bf16[2,2,2,2,32,1344]{5,4,3,2,1,0:T(8,128)(2,1)}, u32[]{:S(2)}, u32[]{:S(2)}) collective-permute-start(bf16[2,2,2,2,32,1344]{5,4,3,2,1,0:T(8,128)(2,1)} %fusion.18), channel_id=1, source_target_pairs={{0,2},{2,0},{4,6},{6,4},{8,10},{10,8},{12,14},{14,12},{16,18},{18,... | collective-permute-start | bytes 4128776 | tf_op jit(solution)/shard_map/ppermute | solution.py:30
  125.0 56.8 %collective-permute-start.30 = (bf16[2,2,2,2,80,384]{5,4,1,2,0,3:T(8,128)(2,1)}, bf16[2,2,2,2,80,384]{5,4,1,2,0,3:T(8,128)(2,1)}, u32[]{:S(2)}, u32[]{:S(2)}) collective-permute-start(bf16[2,2,2,2,80,384]{5,4,1,2,0,3:T(8,128)(2,1)} %bitcast.388), channel_id=1, source_target_pairs={{0,2},{2,0},{4,6},{6,4},{8,10},{10,8},{12,14},{14,12},{16,18},{18,... | collective-permute-start | bytes 2949128 | tf_op jit(solution)/shard_map/ppermute | solution.py:30
  131.6 39.2 %collective-permute-start.35 = (bf16[2,2,2,2,64,384]{5,4,1,2,0,3:T(8,128)(2,1)}, bf16[2,2,2,2,64,384]{5,4,1,2,0,3:T(8,128)(2,1)S(1)}, u32[]{:S(2)}, u32[]{:S(2)}) collective-permute-start(bf16[2,2,2,2,64,384]{5,4,1,2,0,3:T(8,128)(2,1)} %bitcast.424), channel_id=1, source_target_pairs={{0,2},{2,0},{4,6},{6,4},{8,10},{10,8},{12,14},{14,12},{16,18},{18,... | collective-permute-start | bytes 2359304 | tf_op jit(solution)/shard_map/ppermute | solution.py:30
  136.2 7.1 %collective-permute-start.9 = (bf16[1,128,768]{2,1,0:T(8,128)(2,1)S(1)}, bf16[1,128,768]{2,1,0:T(8,128)(2,1)S(1)}, u32[]{:S(2)}, u32[]{:S(2)}) collective-permute-start(bf16[1,128,768]{2,1,0:T(8,128)(2,1)S(1)} %get-tuple-element.28), channel_id=1, source_target_pairs={{0,2},{2,4},{4,6},{6,8},{8,10},{10,12},{12,14},{14,16},{16,18},{18... | collective-permute-start | bytes 589832 | tf_op jit(solution)/shard_map/ppermute | solution.py:15
  143.3 4.6 %collective-permute-start.8 = (bf16[1,128,768]{2,1,0:T(8,128)(2,1)S(1)}, bf16[1,128,768]{2,1,0:T(8,128)(2,1)S(1)}, u32[]{:S(2)}, u32[]{:S(2)}) collective-permute-start(bf16[1,128,768]{2,1,0:T(8,128)(2,1)S(1)} %get-tuple-element.27), channel_id=1, source_target_pairs={{2,0},{4,2},{6,4},{8,6},{10,8},{12,10},{14,12},{16,14},{18,16},{20... | collective-permute-start | bytes 589832 | tf_op jit(solution)/shard_map/ppermute | solution.py:16
  147.9 68.2 %collective-permute-start.20 = (bf16[2,2,2,2,80,384]{5,4,1,2,0,3:T(8,128)(2,1)S(1)}, bf16[2,2,2,2,80,384]{5,4,1,2,0,3:T(8,128)(2,1)S(1)}, u32[]{:S(2)}, u32[]{:S(2)}) collective-permute-start(bf16[2,2,2,2,80,384]{5,4,1,2,0,3:T(8,128)(2,1)S(1)} %bitcast.421), channel_id=1, source_target_pairs={{0,2},{2,0},{4,6},{6,4},{8,10},{10,8},{12,14},{14,12},{16,18},{18,... | collective-permute-start | bytes 2949128 | tf_op jit(solution)/shard_map/ppermute | solution.py:30
  159.8 5.4 %collective-permute-start.50 = (bf16[1,64,768]{2,1,0:T(8,128)(2,1)S(1)}, bf16[1,64,768]{2,1,0:T(8,128)(2,1)S(1)}, u32[]{:S(2)}, u32[]{:S(2)}) collective-permute-start(bf16[1,64,768]{2,1,0:T(8,128)(2,1)S(1)} %get-tuple-element.25), channel_id=1, source_target_pairs={{2,0},{4,2},{6,4},{8,6},{10,8},{12,10},{14,12},{16,14},{18,16},{20... | collective-permute-start | bytes 294920 | tf_op jit(solution)/shard_map/ppermute | solution.py:16
  165.2 74.4 %collective-permute-start.10 = (bf16[2,2,2,2,80,384]{5,4,1,2,0,3:T(8,128)(2,1)S(1)}, bf16[2,2,2,2,80,384]{5,4,1,2,0,3:T(8,128)(2,1)S(1)}, u32[]{:S(2)}, u32[]{:S(2)}) collective-permute-start(bf16[2,2,2,2,80,384]{5,4,1,2,0,3:T(8,128)(2,1)S(1)} %bitcast.420), channel_id=1, source_target_pairs={{0,2},{2,0},{4,6},{6,4},{8,10},{10,8},{12,14},{14,12},{16,18},{18,... | collective-permute-start | bytes 2949128 | tf_op jit(solution)/shard_map/ppermute | solution.py:30
  170.8 10.8 %collective-permute-start.41 = (bf16[2,2,2,16,1344]{4,3,0,1,2:T(8,128)(2,1)S(1)}, bf16[2,2,2,16,1344]{4,3,0,1,2:T(8,128)(2,1)S(1)}, u32[]{:S(2)}, u32[]{:S(2)}) collective-permute-start(bf16[2,2,2,16,1344]{4,3,0,1,2:T(8,128)(2,1)S(1)} %dynamic-slice_bitcast_fusion.8), channel_id=1, source_target_pairs={{0,1},{1,0},{2,3},{3,2},{4,5},{5,4},{6,7},{7,6},{8,9},{9,8},{10,11... | collective-permute-start | bytes 1032200 | tf_op jit(solution)/shard_map/ppermute | solution.py:30
  181.7 27.5 %collective-permute-start.15 = (bf16[2,2,2,2,64,384]{5,4,1,2,0,3:T(8,128)(2,1)S(1)}, bf16[2,2,2,2,64,384]{5,4,1,2,0,3:T(8,128)(2,1)S(1)}, u32[]{:S(2)}, u32[]{:S(2)}) collective-permute-start(bf16[2,2,2,2,64,384]{5,4,1,2,0,3:T(8,128)(2,1)S(1)} %bitcast.426), channel_id=1, source_target_pairs={{0,2},{2,0},{4,6},{6,4},{8,10},{10,8},{12,14},{14,12},{16,18},{18,... | collective-permute-start | bytes 2359304 | tf_op jit(solution)/shard_map/ppermute | solution.py:30
  181.8 7.0 %collective-permute-start.42 = (bf16[2,2,16,1344]{3,2,0,1:T(8,128)(2,1)S(1)}, bf16[2,2,16,1344]{3,2,0,1:T(8,128)(2,1)S(1)}, u32[]{:S(2)}, u32[]{:S(2)}) collective-permute-start(bf16[2,2,16,1344]{3,2,0,1:T(8,128)(2,1)S(1)} %dynamic-slice_bitcast_fusion.16), channel_id=1, source_target_pairs={{0,4},{2,6},{4,0},{6,2},{8,12},{10,14},{12,8},{14,10},{16,20},{18,... | collective-permute-start | bytes 516104 | tf_op jit(solution)/shard_map/ppermute | solution.py:30
  188.9 10.7 %collective-permute-start.36 = (bf16[2,2,2,64,384]{4,3,1,2,0:T(8,128)(2,1)S(1)}, bf16[2,2,2,64,384]{4,3,1,2,0:T(8,128)(2,1)S(1)}, u32[]{:S(2)}, u32[]{:S(2)}) collective-permute-start(bf16[2,2,2,64,384]{4,3,1,2,0:T(8,128)(2,1)S(1)} %dynamic-slice_bitcast_fusion.4), channel_id=1, source_target_pairs={{0,4},{2,6},{4,0},{6,2},{8,12},{10,14},{12,8},{14,10},{16,20},{18,... | collective-permute-start | bytes 1179656 | tf_op jit(solution)/shard_map/ppermute | solution.py:30
  204.2 5.0 %collective-permute-start.44 = (bf16[16,1344]{1,0:T(8,128)(2,1)S(1)}, bf16[16,1344]{1,0:T(8,128)(2,1)S(1)}, u32[]{:S(2)}, u32[]{:S(2)}) collective-permute-start(bf16[16,1344]{1,0:T(8,128)(2,1)S(1)} %dynamic-slice_bitcast_fusion.31), channel_id=1, source_target_pairs={{0,16},{2,18},{4,20},{6,22},{8,24},{10,26},{12,28},{14,30},{16,0},... | collective-permute-start | bytes 129032 | tf_op jit(solution)/shard_map/ppermute | solution.py:30
  209.2 19.1 %collective-permute-start.31 = (bf16[2,2,2,80,384]{4,3,0,1,2:T(8,128)(2,1)S(1)}, bf16[2,2,2,80,384]{4,3,0,1,2:T(8,128)(2,1)S(1)}, u32[]{:S(2)}, u32[]{:S(2)}) collective-permute-start(bf16[2,2,2,80,384]{4,3,0,1,2:T(8,128)(2,1)S(1)} %dynamic-slice_bitcast_fusion.1), channel_id=1, source_target_pairs={{0,1},{1,0},{2,3},{3,2},{4,5},{5,4},{6,7},{7,6},{8,9},{9,8},{10,11... | collective-permute-start | bytes 1474568 | tf_op jit(solution)/shard_map/ppermute | solution.py:30
  211.5 15.7 %collective-permute-start.37 = (bf16[2,2,64,384]{3,2,0,1:T(8,128)(2,1)S(1)}, bf16[2,2,64,384]{3,2,0,1:T(8,128)(2,1)S(1)}, u32[]{:S(2)}, u32[]{:S(2)}) collective-permute-start(bf16[2,2,64,384]{3,2,0,1:T(8,128)(2,1)S(1)} %dynamic-slice_bitcast_fusion.12), channel_id=1, source_target_pairs={{0,1},{1,0},{2,3},{3,2},{4,5},{5,4},{6,7},{7,6},{8,9},{9,8},{10,11... | collective-permute-start | bytes 589832 | tf_op jit(solution)/shard_map/ppermute | solution.py:30
  213.5 40.5 %collective-permute-start.16 = (bf16[2,2,2,64,384]{4,3,1,2,0:T(8,128)(2,1)S(1)}, bf16[2,2,2,64,384]{4,3,1,2,0:T(8,128)(2,1)S(1)}, u32[]{:S(2)}, u32[]{:S(2)}) collective-permute-start(bf16[2,2,2,64,384]{4,3,1,2,0:T(8,128)(2,1)S(1)} %dynamic-slice_bitcast_fusion.6), channel_id=1, source_target_pairs={{0,4},{2,6},{4,0},{6,2},{8,12},{10,14},{12,8},{14,10},{16,20},{18,... | collective-permute-start | bytes 1179656 | tf_op jit(solution)/shard_map/ppermute | solution.py:30
  216.1 39.5 %collective-permute-start.26 = (bf16[2,2,2,64,384]{4,3,1,2,0:T(8,128)(2,1)S(1)}, bf16[2,2,2,64,384]{4,3,1,2,0:T(8,128)(2,1)S(1)}, u32[]{:S(2)}, u32[]{:S(2)}) collective-permute-start(bf16[2,2,2,64,384]{4,3,1,2,0:T(8,128)(2,1)S(1)} %dynamic-slice_bitcast_fusion.5), channel_id=1, source_target_pairs={{0,4},{2,6},{4,0},{6,2},{8,12},{10,14},{12,8},{14,10},{16,20},{18,... | collective-permute-start | bytes 1179656 | tf_op jit(solution)/shard_map/ppermute | solution.py:30
  227.1 48.6 %collective-permute-start.46 = (bf16[2,2,2,32,1344]{4,3,2,1,0:T(8,128)(2,1)S(1)}, bf16[2,2,2,32,1344]{4,3,2,1,0:T(8,128)(2,1)S(1)}, u32[]{:S(2)}, u32[]{:S(2)}) collective-permute-start(bf16[2,2,2,32,1344]{4,3,2,1,0:T(8,128)(2,1)S(1)} %dynamic-slice_bitcast_fusion), channel_id=1, source_target_pairs={{0,4},{2,6},{4,0},{6,2},{8,12},{10,14},{12,8},{14,10},{16,20},{18,... | collective-permute-start | bytes 2064392 | tf_op jit(solution)/shard_map/ppermute | solution.py:30
  228.3 4.7 %collective-permute-start.38 = (bf16[2,64,384]{2,1,0:T(8,128)(2,1)S(1)}, bf16[2,64,384]{2,1,0:T(8,128)(2,1)S(1)}, u32[]{:S(2)}, u32[]{:S(2)}) collective-permute-start(bf16[2,64,384]{2,1,0:T(8,128)(2,1)S(1)} %dynamic-slice_bitcast_fusion.20), channel_id=1, source_target_pairs={{0,8},{2,10},{4,12},{6,14},{8,0},{10,2},{12,4},{14,6},{16,24},{18,... | collective-permute-start | bytes 294920 | tf_op jit(solution)/shard_map/ppermute | solution.py:30
  233.0 5.1 %collective-permute-start.39 = (bf16[64,384]{1,0:T(8,128)(2,1)S(1)}, bf16[64,384]{1,0:T(8,128)(2,1)S(1)}, u32[]{:S(2)}, u32[]{:S(2)}) collective-permute-start(bf16[64,384]{1,0:T(8,128)(2,1)S(1)} %dynamic-slice_bitcast_fusion.28), channel_id=1, source_target_pairs={{0,16},{2,18},{4,20},{6,22},{8,24},{10,26},{12,28},{14,30},{16,0},... | collective-permute-start | bytes 147464 | tf_op jit(solution)/shard_map/ppermute | solution.py:30
  238.1 22.7 %collective-permute-start.21 = (bf16[2,2,2,80,384]{4,3,0,1,2:T(8,128)(2,1)S(1)}, bf16[2,2,2,80,384]{4,3,0,1,2:T(8,128)(2,1)S(1)}, u32[]{:S(2)}, u32[]{:S(2)}) collective-permute-start(bf16[2,2,2,80,384]{4,3,0,1,2:T(8,128)(2,1)S(1)} %dynamic-slice_bitcast_fusion.2), channel_id=1, source_target_pairs={{0,1},{1,0},{2,3},{3,2},{4,5},{5,4},{6,7},{7,6},{8,9},{9,8},{10,11... | collective-permute-start | bytes 1474568 | tf_op jit(solution)/shard_map/ppermute | solution.py:30
  239.6 14.0 %collective-permute-start.32 = (bf16[2,2,80,384]{3,2,0,1:T(8,128)(2,1)S(1)}, bf16[2,2,80,384]{3,2,0,1:T(8,128)(2,1)S(1)}, u32[]{:S(2)}, u32[]{:S(2)}) collective-permute-start(bf16[2,2,80,384]{3,2,0,1:T(8,128)(2,1)S(1)} %dynamic-slice_bitcast_fusion.9), channel_id=1, source_target_pairs={{0,4},{2,6},{4,0},{6,2},{8,12},{10,14},{12,8},{14,10},{16,20},{18,... | collective-permute-start | bytes 737288 | tf_op jit(solution)/shard_map/ppermute | solution.py:30
  253.6 22.8 %collective-permute-start.11 = (bf16[2,2,2,80,384]{4,3,0,1,2:T(8,128)(2,1)S(1)}, bf16[2,2,2,80,384]{4,3,0,1,2:T(8,128)(2,1)S(1)}, u32[]{:S(2)}, u32[]{:S(2)}) collective-permute-start(bf16[2,2,2,80,384]{4,3,0,1,2:T(8,128)(2,1)S(1)} %dynamic-slice_bitcast_fusion.3), channel_id=1, source_target_pairs={{0,1},{1,0},{2,3},{3,2},{4,5},{5,4},{6,7},{7,6},{8,9},{9,8},{10,11... | collective-permute-start | bytes 1474568 | tf_op jit(solution)/shard_map/ppermute | solution.py:30
  254.0 4.9 %collective-permute-start.33 = (bf16[2,80,384]{2,1,0:T(8,128)(2,1)S(1)}, bf16[2,80,384]{2,1,0:T(8,128)(2,1)S(1)}, u32[]{:S(2)}, u32[]{:S(2)}) collective-permute-start(bf16[2,80,384]{2,1,0:T(8,128)(2,1)S(1)} %dynamic-slice_bitcast_fusion.17), channel_id=1, source_target_pairs={{0,8},{2,10},{4,12},{6,14},{8,0},{10,2},{12,4},{14,6},{16,24},{18,... | collective-permute-start | bytes 368648 | tf_op jit(solution)/shard_map/ppermute | solution.py:30
  255.7 16.3 %collective-permute-start.17 = (bf16[2,2,64,384]{3,2,0,1:T(8,128)(2,1)S(1)}, bf16[2,2,64,384]{3,2,0,1:T(8,128)(2,1)S(1)}, u32[]{:S(2)}, u32[]{:S(2)}) collective-permute-start(bf16[2,2,64,384]{3,2,0,1:T(8,128)(2,1)S(1)} %dynamic-slice_bitcast_fusion.14), channel_id=1, source_target_pairs={{0,1},{1,0},{2,3},{3,2},{4,5},{5,4},{6,7},{7,6},{8,9},{9,8},{10,11... | collective-permute-start | bytes 589832 | tf_op jit(solution)/shard_map/ppermute | solution.py:30
  259.0 15.2 %collective-permute-start.27 = (bf16[2,2,64,384]{3,2,0,1:T(8,128)(2,1)S(1)}, bf16[2,2,64,384]{3,2,0,1:T(8,128)(2,1)S(1)}, u32[]{:S(2)}, u32[]{:S(2)}) collective-permute-start(bf16[2,2,64,384]{3,2,0,1:T(8,128)(2,1)S(1)} %dynamic-slice_bitcast_fusion.13), channel_id=1, source_target_pairs={{0,1},{1,0},{2,3},{3,2},{4,5},{5,4},{6,7},{7,6},{8,9},{9,8},{10,11... | collective-permute-start | bytes 589832 | tf_op jit(solution)/shard_map/ppermute | solution.py:30
  260.8 5.2 %collective-permute-start.34 = (bf16[80,384]{1,0:T(8,128)(2,1)S(1)}, bf16[80,384]{1,0:T(8,128)(2,1)S(1)}, u32[]{:S(2)}, u32[]{:S(2)}) collective-permute-start(bf16[80,384]{1,0:T(8,128)(2,1)S(1)} %dynamic-slice_bitcast_fusion.25), channel_id=1, source_target_pairs={{0,16},{2,18},{4,20},{6,22},{8,24},{10,26},{12,28},{14,30},{16,0},... | collective-permute-start | bytes 184328 | tf_op jit(solution)/shard_map/ppermute | solution.py:30
  266.0 14.8 %collective-permute-start.22 = (bf16[2,2,80,384]{3,2,0,1:T(8,128)(2,1)S(1)}, bf16[2,2,80,384]{3,2,0,1:T(8,128)(2,1)S(1)}, u32[]{:S(2)}, u32[]{:S(2)}) collective-permute-start(bf16[2,2,80,384]{3,2,0,1:T(8,128)(2,1)S(1)} %dynamic-slice_bitcast_fusion.10), channel_id=1, source_target_pairs={{0,4},{2,6},{4,0},{6,2},{8,12},{10,14},{12,8},{14,10},{16,20},{18,... | collective-permute-start | bytes 737288 | tf_op jit(solution)/shard_map/ppermute | solution.py:30
  272.1 5.5 %collective-permute-start.18 = (bf16[2,64,384]{2,1,0:T(8,128)(2,1)S(1)}, bf16[2,64,384]{2,1,0:T(8,128)(2,1)S(1)}, u32[]{:S(2)}, u32[]{:S(2)}) collective-permute-start(bf16[2,64,384]{2,1,0:T(8,128)(2,1)S(1)} %dynamic-slice_bitcast_fusion.22), channel_id=1, source_target_pairs={{0,8},{2,10},{4,12},{6,14},{8,0},{10,2},{12,4},{14,6},{16,24},{18,... | collective-permute-start | bytes 294920 | tf_op jit(solution)/shard_map/ppermute | solution.py:30
  274.2 5.2 %collective-permute-start.28 = (bf16[2,64,384]{2,1,0:T(8,128)(2,1)S(1)}, bf16[2,64,384]{2,1,0:T(8,128)(2,1)S(1)}, u32[]{:S(2)}, u32[]{:S(2)}) collective-permute-start(bf16[2,64,384]{2,1,0:T(8,128)(2,1)S(1)} %dynamic-slice_bitcast_fusion.21), channel_id=1, source_target_pairs={{0,8},{2,10},{4,12},{6,14},{8,0},{10,2},{12,4},{14,6},{16,24},{18,... | collective-permute-start | bytes 294920 | tf_op jit(solution)/shard_map/ppermute | solution.py:30
  276.0 17.4 %collective-permute-start.47 = (bf16[2,2,32,1344]{3,2,1,0:T(8,128)(2,1)S(1)}, bf16[2,2,32,1344]{3,2,1,0:T(8,128)(2,1)S(1)}, u32[]{:S(2)}, u32[]{:S(2)}) collective-permute-start(bf16[2,2,32,1344]{3,2,1,0:T(8,128)(2,1)S(1)} %dynamic-slice_bitcast_fusion.7), channel_id=1, source_target_pairs={{0,1},{1,0},{2,3},{3,2},{4,5},{5,4},{6,7},{7,6},{8,9},{9,8},{10,11... | collective-permute-start | bytes 1032200 | tf_op jit(solution)/shard_map/ppermute | solution.py:30
  276.6 15.0 %collective-permute-start.12 = (bf16[2,2,80,384]{3,2,0,1:T(8,128)(2,1)S(1)}, bf16[2,2,80,384]{3,2,0,1:T(8,128)(2,1)S(1)}, u32[]{:S(2)}, u32[]{:S(2)}) collective-permute-start(bf16[2,2,80,384]{3,2,0,1:T(8,128)(2,1)S(1)} %dynamic-slice_bitcast_fusion.11), channel_id=1, source_target_pairs={{0,4},{2,6},{4,0},{6,2},{8,12},{10,14},{12,8},{14,10},{16,20},{18,... | collective-permute-start | bytes 737288 | tf_op jit(solution)/shard_map/ppermute | solution.py:30
  277.7 5.1 %collective-permute-start.19 = (bf16[64,384]{1,0:T(8,128)(2,1)S(1)}, bf16[64,384]{1,0:T(8,128)(2,1)S(1)}, u32[]{:S(2)}, u32[]{:S(2)}) collective-permute-start(bf16[64,384]{1,0:T(8,128)(2,1)S(1)} %dynamic-slice_bitcast_fusion.30), channel_id=1, source_target_pairs={{0,16},{2,18},{4,20},{6,22},{8,24},{10,26},{12,28},{14,30},{16,0},... | collective-permute-start | bytes 147464 | tf_op jit(solution)/shard_map/ppermute | solution.py:30
  279.5 8.8 %collective-permute-start.29 = (bf16[64,384]{1,0:T(8,128)(2,1)S(1)}, bf16[64,384]{1,0:T(8,128)(2,1)S(1)}, u32[]{:S(2)}, u32[]{:S(2)}) collective-permute-start(bf16[64,384]{1,0:T(8,128)(2,1)S(1)} %dynamic-slice_bitcast_fusion.29), channel_id=1, source_target_pairs={{0,16},{2,18},{4,20},{6,22},{8,24},{10,26},{12,28},{14,30},{16,0},... | collective-permute-start | bytes 147464 | tf_op jit(solution)/shard_map/ppermute | solution.py:30
  280.9 5.3 %collective-permute-start.23 = (bf16[2,80,384]{2,1,0:T(8,128)(2,1)S(1)}, bf16[2,80,384]{2,1,0:T(8,128)(2,1)S(1)}, u32[]{:S(2)}, u32[]{:S(2)}) collective-permute-start(bf16[2,80,384]{2,1,0:T(8,128)(2,1)S(1)} %dynamic-slice_bitcast_fusion.18), channel_id=1, source_target_pairs={{0,8},{2,10},{4,12},{6,14},{8,0},{10,2},{12,4},{14,6},{16,24},{18,... | collective-permute-start | bytes 368648 | tf_op jit(solution)/shard_map/ppermute | solution.py:30
  286.3 5.2 %collective-permute-start.24 = (bf16[80,384]{1,0:T(8,128)(2,1)S(1)}, bf16[80,384]{1,0:T(8,128)(2,1)S(1)}, u32[]{:S(2)}, u32[]{:S(2)}) collective-permute-start(bf16[80,384]{1,0:T(8,128)(2,1)S(1)} %dynamic-slice_bitcast_fusion.26), channel_id=1, source_target_pairs={{0,16},{2,18},{4,20},{6,22},{8,24},{10,26},{12,28},{14,30},{16,0},... | collective-permute-start | bytes 184328 | tf_op jit(solution)/shard_map/ppermute | solution.py:30
  291.6 6.4 %collective-permute-start.13 = (bf16[2,80,384]{2,1,0:T(8,128)(2,1)S(1)}, bf16[2,80,384]{2,1,0:T(8,128)(2,1)S(1)}, u32[]{:S(2)}, u32[]{:S(2)}) collective-permute-start(bf16[2,80,384]{2,1,0:T(8,128)(2,1)S(1)} %dynamic-slice_bitcast_fusion.19), channel_id=1, source_target_pairs={{0,8},{2,10},{4,12},{6,14},{8,0},{10,2},{12,4},{14,6},{16,24},{18,... | collective-permute-start | bytes 368648 | tf_op jit(solution)/shard_map/ppermute | solution.py:30
  298.1 7.4 %collective-permute-start.14 = (bf16[80,384]{1,0:T(8,128)(2,1)S(1)}, bf16[80,384]{1,0:T(8,128)(2,1)S(1)}, u32[]{:S(2)}, u32[]{:S(2)}) collective-permute-start(bf16[80,384]{1,0:T(8,128)(2,1)S(1)} %dynamic-slice_bitcast_fusion.27), channel_id=1, source_target_pairs={{0,16},{2,18},{4,20},{6,22},{8,24},{10,26},{12,28},{14,30},{16,0},... | collective-permute-start | bytes 184328 | tf_op jit(solution)/shard_map/ppermute | solution.py:30
  299.8 6.2 %collective-permute-start.48 = (bf16[2,32,1344]{2,1,0:T(8,128)(2,1)S(1)}, bf16[2,32,1344]{2,1,0:T(8,128)(2,1)S(1)}, u32[]{:S(2)}, u32[]{:S(2)}) collective-permute-start(bf16[2,32,1344]{2,1,0:T(8,128)(2,1)S(1)} %dynamic-slice_bitcast_fusion.15), channel_id=1, source_target_pairs={{0,8},{2,10},{4,12},{6,14},{8,0},{10,2},{12,4},{14,6},{16,24},{18,... | collective-permute-start | bytes 516104 | tf_op jit(solution)/shard_map/ppermute | solution.py:30
  306.0 6.5 %collective-permute-start.49 = (bf16[32,1344]{1,0:T(8,128)(2,1)S(1)}, bf16[32,1344]{1,0:T(8,128)(2,1)S(1)}, u32[]{:S(2)}, u32[]{:S(2)}) collective-permute-start(bf16[32,1344]{1,0:T(8,128)(2,1)S(1)} %dynamic-slice_bitcast_fusion.23), channel_id=1, source_target_pairs={{0,16},{2,18},{4,20},{6,22},{8,24},{10,26},{12,28},{14,30},{16,0},... | collective-permute-start | bytes 258056 | tf_op jit(solution)/shard_map/ppermute | solution.py:30
  (38 other events, 219.5 us)

commit v2 on v1

--- a/solution.py
+++ b/solution.py
@@ -1,6 +1,10 @@
+import functools
+
 import jax
 import jax.numpy as jnp
 from jax import lax
+from jax.experimental import pallas as pl
+from jax.experimental.pallas import tpu as pltpu
 from jax.sharding import PartitionSpec as P
 
 OUTPUT_TRACKS = 2688
@@ -126,9 +130,410 @@
     return (loss, jnp.stack(kernel_grads), head_total, stream_grad.astype(jnp.bfloat16))
 
 
+MESH = pl.DeviceIdType.MESH
+TILE = 384
+ORDERS = (("samp", 1, 2, 3), (1, "samp", 2, 3), (2, 3, "samp", 1))
+CONV_CUTS = (0, 64, 128, 144)
+HEAD_CUTS = (0, 16, 32, 48)
+CHUNKS = LAYERS + 1
+STEPS = 4
+FIRST = 4 * LAYERS
+LATER = FIRST + CHUNKS
+LOSS = LATER + CHUNKS * len(ORDERS) * STEPS
+COPIES = LOSS + STEPS + 1
+
+
+def smooth_slope(values):
+    scale = 0.7978845608028654
+    square = values * values
+    bend = jnp.tanh(scale * values * (1.0 + 0.044715 * square))
+    return 0.5 * (1.0 + bend) + 0.5 * values * (1.0 - bend * bend) * scale * (
+        1.0 + 3 * 0.044715 * square
+    )
+
+
+def dot(left, right, left_dim, right_dim):
+    return lax.dot_general(
+        left, right, (((left_dim,), (right_dim,)), ((), ())), preferred_element_type=jnp.float32
+    )
+
+
+def kernel(trunk, conv_hbm, head_hbm, targets_hbm, weights, sums, conv_out, head_out, trunk_out, *scratch):
+    conv_w, head_w, counts, local_sem, send_sem, recv_sem, acts, grads, streams, slopes, stream_grad = scratch[:11]
+    terms, first, later, loss_slots = (
+        scratch[11 : 11 + CHUNKS],
+        scratch[11 + CHUNKS : 11 + 2 * CHUNKS],
+        scratch[11 + 2 * CHUNKS : -1],
+        scratch[-1],
+    )
+    rows, channels = trunk.shape
+    tracks = head_hbm.shape[1]
+    seq, samp = lax.axis_index("seq"), lax.axis_index("samp")
+    last = lax.axis_size("seq") - 1
+    has_left, has_right = seq > 0, seq < last
+    bits = [lax.rem(lax.div(seq, 2**b), 2) for b in range(4)]
+    place = {"samp": samp, **{b: bits[b] for b in range(4)}}
+    partner = {"samp": {"samp": 1 - samp}}
+    for b in range(4):
+        partner[b] = {"seq": seq + (1 - 2 * bits[b]) * 2**b}
+
+    conv_loads = [
+        pltpu.make_async_copy(conv_hbm.at[i], conv_w.at[i], local_sem.at[i]) for i in range(LAYERS)
+    ]
+    head_load = pltpu.make_async_copy(head_hbm, head_w, local_sem.at[LAYERS])
+    count_load = pltpu.make_async_copy(targets_hbm, counts, local_sem.at[LAYERS + 1])
+    for load in conv_loads + [head_load, count_load]:
+        load.start()
+
+    barrier = pltpu.get_barrier_semaphore()
+    right, left = {"seq": seq + 1}, {"seq": seq - 1}
+    for there in (partner["samp"], partner[1], partner[2], partner[3]):
+        pl.semaphore_signal(barrier, inc=1, device_id=there, device_id_type=MESH)
+
+    @pl.when(has_right)
+    def _():
+        pl.semaphore_signal(barrier, inc=1, device_id=right, device_id_type=MESH)
+
+    @pl.when(has_left)
+    def _():
+        pl.semaphore_signal(barrier, inc=1, device_id=left, device_id_type=MESH)
+
+    pl.semaphore_wait(barrier, 4 + has_right.astype(jnp.int32) + has_left.astype(jnp.int32))
+
+    def remote(src, dst, number, there):
+        return pltpu.make_async_remote_copy(
+            src_ref=src,
+            dst_ref=dst,
+            send_sem=send_sem.at[number],
+            recv_sem=recv_sem.at[number],
+            device_id=there,
+            device_id_type=MESH,
+        )
+
+    spreads = [BASE_DILATION * 2**i for i in range(LAYERS)]
+    starts = [sum(rows + 2 * s for s in spreads[:i]) for i in range(LAYERS)]
+
+    def edges(buffer, layer, number):
+        spread, start = spreads[layer], starts[layer]
+        up = remote(
+            buffer.at[pl.ds(start + rows, spread)], buffer.at[pl.ds(start, spread)], number, right
+        )
+        down = remote(
+            buffer.at[pl.ds(start + spread, spread)],
+            buffer.at[pl.ds(start + spread + rows, spread)],
+            number + 1,
+            left,
+        )
+        return up, down
+
+    def send_edges(buffer, layer, number, block):
+        spread, start = spreads[layer], starts[layer]
+        buffer[pl.ds(start + spread, rows)] = block
+        up, down = edges(buffer, layer, number)
+
+        @pl.when(has_right)
+        def _():
+            up.start()
+
+        @pl.when(has_left)
+        def _():
+            down.start()
+
+        @pl.when(jnp.logical_not(has_left))
+        def _():
+            buffer[pl.ds(start, spread)] = jnp.zeros((spread, channels), jnp.bfloat16)
+
+        @pl.when(jnp.logical_not(has_right))
+        def _():
+            buffer[pl.ds(start + spread + rows, spread)] = jnp.zeros((spread, channels), jnp.bfloat16)
+
+    def wait_edges(buffer, layer, number):
+        up, down = edges(buffer, layer, number)
+
+        @pl.when(has_right)
+        def _():
+            up.wait_send()
+            down.wait_recv()
+
+        @pl.when(has_left)
+        def _():
+            down.wait_send()
+            up.wait_recv()
+
+    def view(buffer, layer, tap):
+        return buffer[pl.ds(starts[layer] + tap * spreads[layer], rows)]
+
+    streams[0] = trunk[...]
+    for layer in range(LAYERS):
+        send_edges(
+            acts, layer, 2 * layer, smooth(streams[layer].astype(jnp.float32)).astype(jnp.bfloat16)
+        )
+        conv_loads[layer].wait()
+        total = streams[layer].astype(jnp.float32) + dot(view(acts, layer, 1), conv_w[layer, 1], 1, 0)
+        wait_edges(acts, layer, 2 * layer)
+        for tap in (0, 2):
+            total += dot(view(acts, layer, tap), conv_w[layer, tap], 1, 0)
+        streams[layer + 1] = total.astype(jnp.bfloat16)
+
+    head_load.wait()
+    count_load.wait()
+    stream_grad[...] = jnp.zeros_like(stream_grad)
+
+    def folded(values):
+        return jnp.sum(values.reshape(rows // 8, 8, values.shape[1]), axis=0)
+
+    sums[0:8] = jnp.zeros((8, 128), jnp.float32)
+    sums[8:16] = folded(weights[...])
+
+    def head_tile(step, carry):
+        place_of = pl.ds(pl.multiple_of(step * TILE, 128), TILE)
+        matrix = head_w[:, place_of]
+        logits = dot(streams[LAYERS], matrix, 1, 0)
+        weight = jnp.concatenate([weights[...]] * (TILE // 128), axis=1)
+        tail = jnp.exp(-jnp.abs(logits))
+        predicted = jnp.maximum(logits, 0.0) + jnp.log1p(tail)
+        slope = jnp.where(logits >= 0, 1.0, tail) / (1.0 + tail)
+        seen = counts[:, place_of].astype(jnp.float32)
+        fold = folded(weight * (predicted - seen * jnp.log(predicted)))
+        sums[0:8] += sum(fold[:, i * 128 : (i + 1) * 128] for i in range(TILE // 128))
+        grad = (weight * (1.0 - seen / predicted) * slope).astype(jnp.bfloat16)
+        slopes[:, place_of] = grad
+        stream_grad[...] += dot(grad, matrix, 1, 1)
+        return carry
+
+    lax.fori_loop(0, tracks // TILE, head_tile, 0)
+
+    def first_copy(chunk):
+        return remote(
+            terms[chunk].at[:, :, :, :, 1 - bits[0]], first[chunk], FIRST + chunk, partner[0]
+        )
+
+    def part_rows(chunk, part):
+        cuts = HEAD_CUTS if chunk == 0 else CONV_CUTS
+        return pl.ds(cuts[part], cuts[part + 1] - cuts[part])
+
+    def slot(chunk, part, step):
+        return later[(chunk * len(ORDERS) + part) * STEPS + step]
+
+    def picked(chunk, part, step, which):
+        order = ORDERS[part]
+        labels = ["samp", 3, 2, 1]
+        for done in order[:step]:
+            labels.remove(done)
+        dim = labels.index(order[step])
+        index = place[order[step]] if which == 0 else 1 - place[order[step]]
+        return labels, dim, index
+
+    def later_copy(chunk, part, step):
+        labels, dim, index = picked(chunk, part, step, 1)
+        at = [slice(None)] * len(labels)
+        at[dim] = index
+        if step == 0:
+            src = first[chunk].at[tuple(at) + (part_rows(chunk, part),)]
+        else:
+            src = slot(chunk, part, step - 1).at[tuple(at)]
+        number = LATER + (chunk * len(ORDERS) + part) * STEPS + step
+        return remote(src, slot(chunk, part, step), number, partner[ORDERS[part][step]])
+
+    def added(a, b):
+        return a.astype(jnp.float32) + b.astype(jnp.float32)
+
+    def digits(number, count):
+        return tuple(lax.rem(lax.div(number, 2 ** (count - 1 - i)), 2) for i in range(count))
+
+    def start_later(chunk):
+        first_copy(chunk).wait()
+
+        def add(number, carry):
+            at = digits(number, 4)
+            first[chunk][at] = added(first[chunk][at], terms[chunk][at + (bits[0],)]).astype(
+                jnp.bfloat16
+            )
+            return carry
+
+        lax.fori_loop(0, 16, add, 0)
+        for part in range(len(ORDERS)):
+            later_copy(chunk, part, 0).start()
+
+    def advance(chunk, step):
+        for part in range(len(ORDERS)):
+            later_copy(chunk, part, step).wait()
+            labels, dim, index = picked(chunk, part, step, 0)
+            held = slot(chunk, part, step)
+            before = first[chunk] if step == 0 else slot(chunk, part, step - 1)
+            count = len(labels) - 1
+
+            def values(at):
+                there = at[:dim] + (index,) + at[dim:]
+                if step == 0:
+                    there = there + (part_rows(chunk, part),)
+                return added(held[at] if at else held[...], before[there])
+
+            if step == STEPS - 1:
+                where = part_rows(chunk, part)
+                if chunk == 0:
+                    head_out[where] = values(())
+                else:
+                    conv_out[chunk - 1, where] = values(())
+            else:
+
+                def add(number, carry):
+                    at = digits(number, count)
+                    held[at] = values(at).astype(jnp.bfloat16)
+                    return carry
+
+                lax.fori_loop(0, 2**count, add, 0)
+                later_copy(chunk, part, step + 1).start()
+
+    def loss_copy(step):
+        there = partner[(0, "samp", 1, 2, 3)[step]]
+        return remote(loss_slots.at[2 * step], loss_slots.at[2 * step + 1], LOSS + step, there)
+
+    def loss_start(step):
+        loss_slots[2 * step] = sums[...]
+        loss_copy(step).start()
+
+    def loss_end(step):
+        loss_copy(step).wait()
+        sums[...] += loss_slots[2 * step + 1]
+
+    def put(chunk, value, row, side):
+        size = terms[chunk].shape[5]
+        at = 0
+        while at < value.shape[0]:
+            block, inner = divmod(row + at, size)
+            length = min(size - inner, value.shape[0] - at)
+            where = (side,) + tuple((block >> b) & 1 for b in (3, 2, 1, 0))
+            terms[chunk][where + (pl.ds(inner, length),)] = value[at : at + length].astype(jnp.bfloat16)
+            at += length
+
+    loss_start(0)
+    wide = head_out.shape[1]
+    for side in range(2):
+        base = side * (tracks - wide)
+        for begin in range(0, wide, 512):
+            width = min(512, wide - begin)
+            value = dot(streams[LAYERS], slopes[:, base + begin : base + begin + width], 0, 0)
+            for block in range(16):
+                where = (side,) + tuple((block >> b) & 1 for b in (3, 2, 1, 0))
+                terms[0][where + (slice(None), pl.ds(begin, width))] = value[
+                    block * 48 : (block + 1) * 48
+                ].astype(jnp.bfloat16)
+    first_copy(0).start()
+
+    chunk = 0
+    for layer in reversed(range(LAYERS)):
+        number = 2 * LAYERS + 2 * layer
+        send_edges(grads, layer, number, stream_grad[...].astype(jnp.bfloat16))
+        middle = view(grads, layer, 1)
+        for tap in range(3):
+            for begin in range(0, channels, 384):
+                seen = acts[pl.ds(starts[layer] + tap * spreads[layer], rows), begin : begin + 384]
+                value = dot(seen, middle, 0, 0)
+                for side in range(2):
+                    put(
+                        layer + 1,
+                        value[:, side * channels // 2 : (side + 1) * channels // 2],
+                        tap * channels + begin,
+                        side,
+                    )
+        first_copy(layer + 1).start()
+        start_later(chunk)
+        chunk = layer + 1
+        loss_end(LAYERS - 1 - layer)
+        loss_start(LAYERS - layer)
+        total = dot(middle, conv_w[layer, 1], 1, 1)
+        wait_edges(grads, layer, number)
+        for tap in (0, 2):
+            total += dot(view(grads, layer, 2 - tap), conv_w[layer, tap], 1, 1)
+        stream_grad[...] += smooth_slope(streams[layer].astype(jnp.float32)) * total
+    start_later(1)
+    trunk_out[...] = stream_grad[...]
+    loss_end(3)
+    loss_start(4)
+    turns = ((0, 0), (3, 0), (0, 1), (2, 0), (3, 1), (0, 2), (1, 0), (2, 1), (3, 2), (0, 3), (1, 1), (2, 2), (3, 3), (1, 2), (2, 3), (1, 3))
+    for chunk, step in turns:
+        advance(chunk, step)
+    loss_end(4)
+
+
+def per_device_kernel(trunk, conv_weight, head_weight, targets, error_mask, upweight):
+    windows, rows, channels = trunk.shape
+    devices = lax.axis_size("seq")
+    tracks = head_weight.shape[1]
+    bins_all = windows * rows * devices * lax.axis_size("samp")
+    bin_weight = jnp.where(error_mask == 1, upweight, 1).astype(jnp.float32)
+    spreads = [BASE_DILATION * 2**i for i in range(LAYERS)]
+    extended_rows = sum(rows + 2 * s for s in spreads)
+    half = tracks // 2
+    wide = (half + 127) // 128 * 128
+    sizes = [(channels // devices, wide)] + [(3 * channels // devices, channels // 2)] * LAYERS
+    cuts = [HEAD_CUTS] + [CONV_CUTS] * LAYERS
+    vmem = functools.partial(pltpu.VMEM, dtype=jnp.bfloat16)
+    scratch = [
+        vmem(conv_weight.shape),
+        vmem(head_weight.shape),
+        pltpu.VMEM((rows, tracks), jnp.int32),
+        pltpu.SemaphoreType.DMA((LAYERS + 2,)),
+        pltpu.SemaphoreType.DMA((COPIES,)),
+        pltpu.SemaphoreType.DMA((COPIES,)),
+        vmem((extended_rows, channels)),
+        vmem((extended_rows, channels)),
+        vmem((LAYERS + 1, rows, channels)),
+        vmem((rows, tracks)),
+        pltpu.VMEM((rows, channels), jnp.float32),
+    ]
+    scratch += [vmem((2,) * 5 + size) for size in sizes]
+    scratch += [vmem((2,) * 4 + size) for size in sizes]
+    for size, cut in zip(sizes, cuts):
+        for part in range(len(ORDERS)):
+            for step in range(STEPS):
+                scratch.append(vmem((2,) * (3 - step) + (cut[part + 1] - cut[part], size[1])))
+    scratch.append(pltpu.VMEM((2 * (STEPS + 1), 16, 128), jnp.float32))
+    whole = pl.BlockSpec(memory_space=pltpu.VMEM)
+    away = pl.BlockSpec(memory_space=pl.ANY)
+    sums, conv_grad, head_grad, trunk_grad = pl.pallas_call(
+        kernel,
+        out_shape=(
+            jax.ShapeDtypeStruct((16, 128), jnp.float32),
+            jax.ShapeDtypeStruct((LAYERS,) + sizes[1], jnp.float32),
+            jax.ShapeDtypeStruct(sizes[0], jnp.float32),
+            jax.ShapeDtypeStruct((rows, channels), jnp.float32),
+        ),
+        in_specs=[whole, away, away, away, whole],
+        out_specs=(whole,) * 4,
+        scratch_shapes=scratch,
+        compiler_params=pltpu.CompilerParams(
+            collective_id=0, has_side_effects=True, vmem_limit_bytes=63 * 2**20
+        ),
+    )(
+        trunk.reshape(rows, channels),
+        conv_weight,
+        head_weight,
+        targets.reshape(rows, tracks),
+        jnp.broadcast_to(bin_weight.reshape(rows, 1), (rows, 128)),
+    )
+    weight_sum = jnp.sum(sums[8:16, 0])
+    loss = jnp.sum(sums[0:8]) / (OUTPUT_TRACKS * weight_sum)
+    factor = bins_all / weight_sum
+    head_grad = lax.dynamic_slice_in_dim(
+        head_grad, lax.axis_index("samp") * (wide - half), half, axis=1
+    )
+    return (
+        loss,
+        conv_grad * factor,
+        head_grad * factor,
+        (trunk_grad * factor).astype(jnp.bfloat16).reshape(trunk.shape),
+    )
+
+
+def fits(mesh):
+    return mesh.shape["seq"] == 16 and mesh.shape["samp"] == 2
+
+
 def solution(mesh):
     return jax.shard_map(
-        per_device,
+        per_device_kernel if fits(mesh) else per_device,
         mesh=mesh,
         in_specs=(
             P("samp", "seq", None),

time: 315 us -> 136 us (0.43)
  Pallas kernels: 0 us -> 122 us
  waiting for transfers between devices: 101 us -> 0 us
  starting transfers between devices: 83.9 us -> 0 us
  blocking collectives: 47.2 us -> 0 us
  matrix products: 36.6 us -> 0 us
  local copies, waits for them, and re-layouts: 19.7 us -> 0.76 us
  other arithmetic: 20.9 us -> 8.96 us
    pallas_call x0 -> x1, Pallas kernels: none -> 122 us  [per_device_kernel(): pl.pallas_call(kernel, out_shape=(jax.ShapeDtypeStruct((16, 128), jnp.flo...]
    ppermute x52 -> x0, waiting for transfers between devices: 101 us -> none  [the longest x40 89.8 us: halve(): come = lax.ppermute(away, axis, pairs)]
    ppermute x52 -> x0, starting transfers between devices: 83.9 us -> none  [the longest x40 54.9 us: halve(): come = lax.ppermute(away, axis, pairs)]
    psum x1 -> x0, blocking collectives: 47.2 us -> none  [per_device(): loss_sum = lax.psum(partial_loss, ('seq', 'samp'))]
    dot_general x22 -> x0, matrix products: 36.6 us -> none  [the longest x9 11.7 us: per_device(): jnp.dot(view.reshape(row_count, channels), conv_weight[layer_number, k].T...]
    convert_element_type x37 -> x1, other arithmetic: 13.5 us -> 0.7 us  [per_device_kernel(): bin_weight = jnp.where(error_mask == 1, upweight, 1).astype(jnp.float32)]
    convert_element_type x2 -> x0, local copies, waits for them, and re-layouts: 7.03 us -> none  [per_device(): jnp.dot(residual_rows.T, part, preferred_element_type=jnp.float32)]
    unnamed x75 -> x0, local copies, waits for them, and re-layouts: 6.5 us -> none
  transfers between devices with their start and end apart: 52 -> 0, of which waited for: 26 -> 0; matrix products, arithmetic and copies ran while one was open for 17% -> 0% of each run, Pallas kernels for 0% -> 0%
where the time goes in v2:
time: 136 us
  Pallas kernels  122 us (90%)
  other arithmetic  8.96 us (7%)
  between operations  3.77 us (3%)
    pallas_call x1, Pallas kernels, per_device_kernel(): pl.pallas_call(kernel, out_shape=(jax.ShapeDtypeStruct((16, 128), jnp.flo...  122 us

profile of v2, /device:TPU:0, one launch (start us, length us, event | category | flops | bytes accessed | tf_op | source)
XLA Modules:
  0.0 135.9 jit_solution(817718103250609538)
XLA Ops:
  0.6 0.7 fusion.1
  1.3 0.8 broadcast_in_dim.10.weights
  2.1 122.4 %shard_map.93 = (f32[16,128]{1,0:T(8,128)}, f32[3,144,384]{2,1,0:T(8,128)}, f32[48,1408]{1,0:T(8,128)}, f32[256,768]{1,0:T(8,128)}) custom-call(bf16[256,768]{1,0:T(8,128)(2,1)} %bitcast.6, bf16[3,3,768,768]{3,2,1,0:T(8,128)(2,1)} %conv_hbm.1, bf16[768,2688]{1,0:T(8,128)(2,1)} %head_hbm.1, s32[256,2688]{1,0:T(8,128)} %bitcast.5, ...), custom_call_target="tpu_custom_call" | custom-call | tf_op jit(solution)/shard_map/pallas_call | solution.py:495
  124.5 1.3 slice_reduce_fusion
  126.5 1.8 %dynamic-slice_multiply_fusion = f32[48,1344]{1,0:T(8,128)} fusion(f32[48,1408]{1,0:T(8,128)} %get-tuple-element.10, s32[]{:T(128)S(6)} %select_n.8, f32[]{:T(128)S(6)} %div.7), kind=kLoop, calls=%fused_computation.3 | loop fusion | flops 64512 | bytes 516104 | tf_op jit(solution)/shard_map/mul | solution.py:525
  128.3 1.9 %fusion = bf16[1,256,768]{2,1,0:T(8,128)(2,1)} fusion(f32[256,768]{1,0:T(8,128)} %get-tuple-element.11, f32[]{:T(128)S(6)} %div.7), kind=kLoop, calls=%fused_computation.1 | loop fusion | flops 393216 | bytes 1179652 | tf_op jit(solution)/shard_map/reshape | solution.py:526
  130.2 2.0 %broadcast_multiply_fusion = f32[3,144,384]{2,1,0:T(8,128)} fusion(f32[3,144,384]{2,1,0:T(8,128)} %get-tuple-element.9, f32[]{:T(128)S(6)} %div.7), kind=kLoop, calls=%fused_computation.2 | loop fusion | flops 165888 | bytes 1327108 | tf_op jit(solution)/shard_map/mul | solution.py:524
  132.8 1.3 slice_reduce_fusion.1

commit v3 on v2

--- a/solution.py
+++ b/solution.py
@@ -133,9 +133,21 @@
 MESH = pl.DeviceIdType.MESH
 TILE = 384
 ORDERS = (("samp", 1, 2, 3), (1, "samp", 2, 3), (2, 3, "samp", 1))
-CONV_CUTS = (0, 64, 128, 144)
-HEAD_CUTS = (0, 16, 32, 48)
+CUTS = ((0, 16, 32, 48), (0, 48, 96, 144), (0, 64, 128, 144), (0, 64, 128, 144))
 CHUNKS = LAYERS + 1
+TURNS = {
+    0: (),
+    3: ((0, 0, 0), (0, 1, 0), (0, 2, 0), (3, 2, 0)),
+    2: ((3, 0, 0), (3, 1, 0), (2, 2, 0)),
+    1: (
+        (0, 2, 1), (3, 2, 1), (2, 0, 0), (2, 1, 0), (0, 0, 1), (0, 1, 1), (1, 2, 0), (2, 2, 1),
+        (0, 0, 2), (0, 1, 2), (1, 0, 0), (1, 1, 0), (1, 2, 1), (0, 0, 3), (3, 0, 1), (3, 1, 1),
+        (0, 1, 3), (0, 2, 2), (3, 2, 2), (3, 0, 2), (2, 0, 1), (3, 1, 2), (2, 1, 1), (3, 0, 3),
+        (2, 2, 2), (1, 0, 1), (0, 2, 3), (3, 2, 3), (2, 0, 2), (2, 2, 3), (3, 1, 3), (1, 1, 1),
+        (1, 2, 2), (2, 1, 2), (1, 0, 2), (1, 2, 3), (2, 0, 3), (1, 1, 2), (2, 1, 3), (1, 0, 3),
+        (1, 1, 3),
+    ),
+}
 STEPS = 4
 FIRST = 4 * LAYERS
 LATER = FIRST + CHUNKS
@@ -158,8 +170,12 @@
     )
 
 
-def kernel(trunk, conv_hbm, head_hbm, targets_hbm, weights, sums, conv_out, head_out, trunk_out, *scratch):
-    conv_w, head_w, counts, local_sem, send_sem, recv_sem, acts, grads, streams, slopes, stream_grad = scratch[:11]
+def kernel(
+    trunk, conv_hbm, head_hbm, targets_hbm, mask, upweight, loss_out, conv_out, head_out, trunk_out, *scratch
+):
+    conv_w, head_w, counts, local_sem, send_sem, recv_sem, acts, grads, streams, slopes = scratch[:10]
+    stream_grad, weights, sums, turned = scratch[10:14]
+    scratch = scratch[3:]
     terms, first, later, loss_slots = (
         scratch[11 : 11 + CHUNKS],
         scratch[11 + CHUNKS : 11 + 2 * CHUNKS],
@@ -184,6 +200,11 @@
     count_load = pltpu.make_async_copy(targets_hbm, counts, local_sem.at[LAYERS + 1])
     for load in conv_loads + [head_load, count_load]:
         load.start()
+
+    streams[0] = trunk[...]
+    first_act = smooth(trunk[...].astype(jnp.float32)).astype(jnp.bfloat16)
+    row = jnp.where(mask[...] == 1, upweight[...], 1).astype(jnp.float32)
+    weights[...] = jnp.broadcast_to(row, (128, rows)).T
 
     barrier = pltpu.get_barrier_semaphore()
     right, left = {"seq": seq + 1}, {"seq": seq - 1}
@@ -263,11 +284,11 @@
     def view(buffer, layer, tap):
         return buffer[pl.ds(starts[layer] + tap * spreads[layer], rows)]
 
-    streams[0] = trunk[...]
     for layer in range(LAYERS):
-        send_edges(
-            acts, layer, 2 * layer, smooth(streams[layer].astype(jnp.float32)).astype(jnp.bfloat16)
-        )
+        block = first_act
+        if layer > 0:
+            block = smooth(streams[layer].astype(jnp.float32)).astype(jnp.bfloat16)
+        send_edges(acts, layer, 2 * layer, block)
         conv_loads[layer].wait()
         total = streams[layer].astype(jnp.float32) + dot(view(acts, layer, 1), conv_w[layer, 1], 1, 0)
         wait_edges(acts, layer, 2 * layer)
@@ -277,31 +298,10 @@
 
     head_load.wait()
     count_load.wait()
-    stream_grad[...] = jnp.zeros_like(stream_grad)
+    turned[...] = streams[LAYERS][...].T
 
     def folded(values):
         return jnp.sum(values.reshape(rows // 8, 8, values.shape[1]), axis=0)
-
-    sums[0:8] = jnp.zeros((8, 128), jnp.float32)
-    sums[8:16] = folded(weights[...])
-
-    def head_tile(step, carry):
-        place_of = pl.ds(pl.multiple_of(step * TILE, 128), TILE)
-        matrix = head_w[:, place_of]
-        logits = dot(streams[LAYERS], matrix, 1, 0)
-        weight = jnp.concatenate([weights[...]] * (TILE // 128), axis=1)
-        tail = jnp.exp(-jnp.abs(logits))
-        predicted = jnp.maximum(logits, 0.0) + jnp.log1p(tail)
-        slope = jnp.where(logits >= 0, 1.0, tail) / (1.0 + tail)
-        seen = counts[:, place_of].astype(jnp.float32)
-        fold = folded(weight * (predicted - seen * jnp.log(predicted)))
-        sums[0:8] += sum(fold[:, i * 128 : (i + 1) * 128] for i in range(TILE // 128))
-        grad = (weight * (1.0 - seen / predicted) * slope).astype(jnp.bfloat16)
-        slopes[:, place_of] = grad
-        stream_grad[...] += dot(grad, matrix, 1, 1)
-        return carry
-
-    lax.fori_loop(0, tracks // TILE, head_tile, 0)
 
     def first_copy(chunk):
         return remote(
@@ -309,8 +309,7 @@
         )
 
     def part_rows(chunk, part):
-        cuts = HEAD_CUTS if chunk == 0 else CONV_CUTS
-        return pl.ds(cuts[part], cuts[part + 1] - cuts[part])
+        return pl.ds(CUTS[chunk][part], CUTS[chunk][part + 1] - CUTS[chunk][part])
 
     def slot(chunk, part, step):
         return later[(chunk * len(ORDERS) + part) * STEPS + step]
@@ -355,35 +354,44 @@
         for part in range(len(ORDERS)):
             later_copy(chunk, part, 0).start()
 
-    def advance(chunk, step):
-        for part in range(len(ORDERS)):
-            later_copy(chunk, part, step).wait()
-            labels, dim, index = picked(chunk, part, step, 0)
-            held = slot(chunk, part, step)
-            before = first[chunk] if step == 0 else slot(chunk, part, step - 1)
-            count = len(labels) - 1
-
-            def values(at):
-                there = at[:dim] + (index,) + at[dim:]
-                if step == 0:
-                    there = there + (part_rows(chunk, part),)
-                return added(held[at] if at else held[...], before[there])
-
-            if step == STEPS - 1:
-                where = part_rows(chunk, part)
-                if chunk == 0:
-                    head_out[where] = values(())
-                else:
-                    conv_out[chunk - 1, where] = values(())
+    def advance(chunk, part, step):
+        later_copy(chunk, part, step).wait()
+        labels, dim, index = picked(chunk, part, step, 0)
+        held = slot(chunk, part, step)
+        before = first[chunk] if step == 0 else slot(chunk, part, step - 1)
+        count = len(labels) - 1
+
+        def values(at):
+            there = at[:dim] + (index,) + at[dim:]
+            if step == 0:
+                there = there + (part_rows(chunk, part),)
+            return added(held[at] if at else held[...], before[there])
+
+        if step == STEPS - 1:
+            where = part_rows(chunk, part)
+            total = values(()) * factor()
+            if chunk == 0:
+                half = head_out.shape[1]
+                moved = pltpu.roll(total, half, axis=1)
+                head_out[where] = jnp.where(samp == 1, moved, total)[:, :half]
             else:
-
-                def add(number, carry):
-                    at = digits(number, count)
-                    held[at] = values(at).astype(jnp.bfloat16)
-                    return carry
-
-                lax.fori_loop(0, 2**count, add, 0)
-                later_copy(chunk, part, step + 1).start()
+                conv_out[chunk - 1, where] = total
+        else:
+
+            def add(number, carry):
+                at = digits(number, count)
+                held[at] = values(at).astype(jnp.bfloat16)
+                return carry
+
+            lax.fori_loop(0, 2**count, add, 0)
+            later_copy(chunk, part, step + 1).start()
+
+    def weight_sum():
+        return jnp.sum(sums[8:16, 0:1], axis=0, keepdims=True)
+
+    def factor():
+        bins_all = float(rows) * lax.axis_size("seq") * lax.axis_size("samp")
+        return bins_all / weight_sum()
 
     def loss_copy(step):
         there = partner[(0, "samp", 1, 2, 3)[step]]
@@ -407,19 +415,43 @@
             terms[chunk][where + (pl.ds(inner, length),)] = value[at : at + length].astype(jnp.bfloat16)
             at += length
 
+    wide = terms[0].shape[6]
+    loss_fold = jnp.zeros((8, 128), jnp.float32)
+    for tile in range(tracks // TILE):
+        begin = tile * TILE
+        matrix = head_w[:, begin : begin + TILE]
+        logits = dot(streams[LAYERS], matrix, 1, 0)
+        weight = jnp.concatenate([weights[...]] * (TILE // 128), axis=1)
+        tail = jnp.exp(-jnp.abs(logits))
+        above = 1.0 + tail
+        inverse = 1.0 / above
+        predicted = jnp.maximum(logits, 0.0) + (jnp.log(above) + (tail - (above - 1.0)) * inverse)
+        slope = jnp.where(logits >= 0, 1.0, tail) * inverse
+        seen = counts[:, begin : begin + TILE].astype(jnp.float32)
+        fold = folded(weight * (predicted - seen * jnp.log(predicted)))
+        loss_fold += sum(fold[:, i * 128 : (i + 1) * 128] for i in range(TILE // 128))
+        grad = (weight * (1.0 - seen / predicted) * slope).astype(jnp.bfloat16)
+        slopes[:, begin : begin + TILE] = grad
+        value = dot(turned[...], grad, 1, 0).astype(jnp.bfloat16)
+        for side in range(2):
+            base = side * (tracks - wide)
+            low, high = max(begin, base), min(begin + TILE, base + wide)
+            if low < high:
+                for block in range(16):
+                    where = (side,) + tuple((block >> b) & 1 for b in (3, 2, 1, 0))
+                    terms[0][where + (slice(None), pl.ds(low - base, high - low))] = value[
+                        block * 48 : (block + 1) * 48, low - begin : high - begin
+                    ]
+    first_copy(0).start()
+    sums[0:8] = loss_fold
+    sums[8:16] = folded(weights[...])
     loss_start(0)
-    wide = head_out.shape[1]
-    for side in range(2):
-        base = side * (tracks - wide)
-        for begin in range(0, wide, 512):
-            width = min(512, wide - begin)
-            value = dot(streams[LAYERS], slopes[:, base + begin : base + begin + width], 0, 0)
-            for block in range(16):
-                where = (side,) + tuple((block >> b) & 1 for b in (3, 2, 1, 0))
-                terms[0][where + (slice(None), pl.ds(begin, width))] = value[
-                    block * 48 : (block + 1) * 48
-                ].astype(jnp.bfloat16)
-    first_copy(0).start()
+    stream_grad[...] = dot(slopes[...], head_w[...], 1, 1)
+
+    def begin_and_turn(chunk):
+        start_later(chunk)
+        for turn in TURNS[chunk]:
+            advance(*turn)
 
     chunk = 0
     for layer in reversed(range(LAYERS)):
@@ -438,7 +470,7 @@
                         side,
                     )
         first_copy(layer + 1).start()
-        start_later(chunk)
+        begin_and_turn(chunk)
         chunk = layer + 1
         loss_end(LAYERS - 1 - layer)
         loss_start(LAYERS - layer)
@@ -447,28 +479,27 @@
         for tap in (0, 2):
             total += dot(view(grads, layer, 2 - tap), conv_w[layer, tap], 1, 1)
         stream_grad[...] += smooth_slope(streams[layer].astype(jnp.float32)) * total
-    start_later(1)
-    trunk_out[...] = stream_grad[...]
     loss_end(3)
     loss_start(4)
-    turns = ((0, 0), (3, 0), (0, 1), (2, 0), (3, 1), (0, 2), (1, 0), (2, 1), (3, 2), (0, 3), (1, 1), (2, 2), (3, 3), (1, 2), (2, 3), (1, 3))
-    for chunk, step in turns:
-        advance(chunk, step)
+    start_later(1)
     loss_end(4)
+    trunk_out[...] = (stream_grad[...] * factor()).astype(jnp.bfloat16)
+    loss_out[...] = jnp.sum(
+        jnp.sum(sums[0:8], axis=0, keepdims=True), axis=1, keepdims=True
+    ) / (OUTPUT_TRACKS * weight_sum())
+    for turn in TURNS[1]:
+        advance(*turn)
 
 
 def per_device_kernel(trunk, conv_weight, head_weight, targets, error_mask, upweight):
     windows, rows, channels = trunk.shape
     devices = lax.axis_size("seq")
     tracks = head_weight.shape[1]
-    bins_all = windows * rows * devices * lax.axis_size("samp")
-    bin_weight = jnp.where(error_mask == 1, upweight, 1).astype(jnp.float32)
     spreads = [BASE_DILATION * 2**i for i in range(LAYERS)]
     extended_rows = sum(rows + 2 * s for s in spreads)
     half = tracks // 2
     wide = (half + 127) // 128 * 128
     sizes = [(channels // devices, wide)] + [(3 * channels // devices, channels // 2)] * LAYERS
-    cuts = [HEAD_CUTS] + [CONV_CUTS] * LAYERS
     vmem = functools.partial(pltpu.VMEM, dtype=jnp.bfloat16)
     scratch = [
         vmem(conv_weight.shape),
@@ -482,25 +513,28 @@
         vmem((LAYERS + 1, rows, channels)),
         vmem((rows, tracks)),
         pltpu.VMEM((rows, channels), jnp.float32),
+        pltpu.VMEM((rows, 128), jnp.float32),
+        pltpu.VMEM((16, 128), jnp.float32),
+        vmem((channels, rows)),
     ]
     scratch += [vmem((2,) * 5 + size) for size in sizes]
     scratch += [vmem((2,) * 4 + size) for size in sizes]
-    for size, cut in zip(sizes, cuts):
+    for size, cut in zip(sizes, CUTS):
         for part in range(len(ORDERS)):
             for step in range(STEPS):
                 scratch.append(vmem((2,) * (3 - step) + (cut[part + 1] - cut[part], size[1])))
     scratch.append(pltpu.VMEM((2 * (STEPS + 1), 16, 128), jnp.float32))
     whole = pl.BlockSpec(memory_space=pltpu.VMEM)
     away = pl.BlockSpec(memory_space=pl.ANY)
-    sums, conv_grad, head_grad, trunk_grad = pl.pallas_call(
+    loss, conv_grad, head_grad, trunk_grad = pl.pallas_call(
         kernel,
         out_shape=(
-            jax.ShapeDtypeStruct((16, 128), jnp.float32),
+            jax.ShapeDtypeStruct((1, 1), jnp.float32),
             jax.ShapeDtypeStruct((LAYERS,) + sizes[1], jnp.float32),
-            jax.ShapeDtypeStruct(sizes[0], jnp.float32),
-            jax.ShapeDtypeStruct((rows, channels), jnp.float32),
+            jax.ShapeDtypeStruct((sizes[0][0], half), jnp.float32),
+            jax.ShapeDtypeStruct((rows, channels), jnp.bfloat16),
         ),
-        in_specs=[whole, away, away, away, whole],
+        in_specs=[whole, away, away, away, whole, whole],
         out_specs=(whole,) * 4,
         scratch_shapes=scratch,
         compiler_params=pltpu.CompilerParams(
@@ -511,20 +545,10 @@
         conv_weight,
         head_weight,
         targets.reshape(rows, tracks),
-        jnp.broadcast_to(bin_weight.reshape(rows, 1), (rows, 128)),
-    )
-    weight_sum = jnp.sum(sums[8:16, 0])
-    loss = jnp.sum(sums[0:8]) / (OUTPUT_TRACKS * weight_sum)
-    factor = bins_all / weight_sum
-    head_grad = lax.dynamic_slice_in_dim(
-        head_grad, lax.axis_index("samp") * (wide - half), half, axis=1
-    )
-    return (
-        loss,
-        conv_grad * factor,
-        head_grad * factor,
-        (trunk_grad * factor).astype(jnp.bfloat16).reshape(trunk.shape),
-    )
+        error_mask,
+        upweight,
+    )
+    return loss.reshape(()), conv_grad, head_grad, trunk_grad.reshape(trunk.shape)
 
 
 def fits(mesh):

time: 136 us -> 129 us (0.949)
  other arithmetic: 8.96 us -> 0 us
  local copies, waits for them, and re-layouts: 0.76 us -> 5.41 us
  between operations: 3.77 us -> 2.34 us
    unnamed x0 -> x3, local copies, waits for them, and re-layouts: none -> 5.41 us
    mul x2 -> x0, other arithmetic: 3.77 us -> none  [the longest x1 1.97 us: per_device_kernel(): conv_grad * factor]
    reduce_sum x2 -> x0, other arithmetic: 2.56 us -> none  [the longest x1 1.29 us: per_device_kernel(): loss = jnp.sum(sums[0:8]) / (OUTPUT_TRACKS * weight_sum)]
    reshape x1 -> x0, other arithmetic: 1.92 us -> none  [per_device_kernel(): (trunk_grad * factor).astype(jnp.bfloat16).reshape(trunk.shape)]
    pallas_call x1, Pallas kernels: 122 us -> 121 us  [per_device_kernel(): pl.pallas_call(kernel, out_shape=(jax.ShapeDtypeStruct((1, 1), jnp.float3...]
where the time goes in v3:
time: 129 us
  Pallas kernels  121 us (94%)
  local copies, waits for them, and re-layouts  5.41 us (4%)
  between operations  2.34 us (2%)
    pallas_call x1, Pallas kernels, per_device_kernel(): pl.pallas_call(kernel, out_shape=(jax.ShapeDtypeStruct((1, 1), jnp.float3...  121 us
    unnamed x3, local copies, waits for them, and re-layouts  5.41 us

profile of v3, /device:TPU:0, one launch (start us, length us, event | category | flops | bytes accessed | tf_op | source)
XLA Modules:
  0.0 128.7 jit_solution(17339726287966234261)
XLA Ops:
  0.6 121.0 %shard_map.93 = (f32[1,1]{1,0:T(1,128)}, f32[3,144,384]{2,1,0:T(8,128)}, f32[48,1344]{1,0:T(8,128)}, bf16[256,768]{1,0:T(8,128)(2,1)}) custom-call(bf16[256,768]{1,0:T(8,128)(2,1)} %bitcast.6, bf16[3,3,768,768]{3,2,1,0:T(8,128)(2,1)} %conv_hbm.1, bf16[768,2688]{1,0:T(8,128)(2,1)} %head_hbm.1, s32[256,2688]{1,0:T(8,128)} %bitcast.4, s32[1,256]{1,0:T(1,128)} %mask.1, ...), custom_call_target="tpu_custom_call" | custom-call | tf_op jit(solution)/shard_map/pallas_call | solution.py:529
  122.2 2.0 %copy.15 = f32[3,144,384]{2,1,0:T(8,128)} copy(f32[3,144,384]{2,1,0:T(8,128)} %get-tuple-element.17) | data formatting | bytes 1327104
  124.2 1.7 %copy.16 = f32[48,1344]{1,0:T(8,128)} copy(f32[48,1344]{1,0:T(8,128)} %get-tuple-element.18) | data formatting | bytes 516096
  125.8 1.8 %copy.17 = bf16[1,256,768]{2,1,0:T(8,128)(2,1)} copy(bf16[1,256,768]{2,1,0:T(8,128)(2,1)} %bitcast.5) | data formatting | bytes 786432

commit v4 on v3

--- a/solution.py
+++ b/solution.py
@@ -132,27 +132,41 @@
 
 MESH = pl.DeviceIdType.MESH
 TILE = 384
-ORDERS = (("samp", 1, 2, 3), (1, "samp", 2, 3), (2, 3, "samp", 1))
-CUTS = ((0, 16, 32, 48), (0, 48, 96, 144), (0, 64, 128, 144), (0, 64, 128, 144))
+ORDERS = (
+    (("samp", 1, 2, 3), (1, "samp", 2, 3), (2, 3, "samp", 1)),
+    ((1, 2, 3), (1, 2, 3), (1, 2, 3)),
+    ((1, 2, 3), (2, 3, 1)),
+    ((1, 2, 3), (2, 3, 1)),
+)
+LABELS = (("samp", 3, 2, 1), (3, 2, 1), (3, 2, 1), (3, 2, 1))
+CUTS = ((0, 16, 32, 48), (0, 48, 96, 144), (0, 128, 144), (0, 80, 144))
 CHUNKS = LAYERS + 1
 TURNS = {
-    0: (),
-    3: ((0, 0, 0), (0, 1, 0), (0, 2, 0), (3, 2, 0)),
-    2: ((3, 0, 0), (3, 1, 0), (2, 2, 0)),
+    0: (
+    ),
+    3: (
+    ),
+    2: (
+        (0, 0, 0), (0, 1, 0), (0, 2, 0), (3, 1, 0), (3, 0, 0),
+    ),
     1: (
-        (0, 2, 1), (3, 2, 1), (2, 0, 0), (2, 1, 0), (0, 0, 1), (0, 1, 1), (1, 2, 0), (2, 2, 1),
-        (0, 0, 2), (0, 1, 2), (1, 0, 0), (1, 1, 0), (1, 2, 1), (0, 0, 3), (3, 0, 1), (3, 1, 1),
-        (0, 1, 3), (0, 2, 2), (3, 2, 2), (3, 0, 2), (2, 0, 1), (3, 1, 2), (2, 1, 1), (3, 0, 3),
-        (2, 2, 2), (1, 0, 1), (0, 2, 3), (3, 2, 3), (2, 0, 2), (2, 2, 3), (3, 1, 3), (1, 1, 1),
-        (1, 2, 2), (2, 1, 2), (1, 0, 2), (1, 2, 3), (2, 0, 3), (1, 1, 2), (2, 1, 3), (1, 0, 3),
-        (1, 1, 3),
+        (2, 1, 0), (0, 1, 1), (0, 2, 1), (3, 1, 1), (2, 0, 0), (3, 0, 1),
+        (2, 1, 1), (0, 2, 2), (0, 0, 1), (0, 1, 2), (1, 0, 0), (2, 0, 1),
+        (3, 0, 2), (1, 1, 0), (0, 0, 2), (0, 1, 3), (1, 2, 0), (1, 0, 1),
+        (3, 1, 2), (2, 1, 2), (0, 2, 3), (2, 0, 2), (1, 1, 1), (0, 0, 3),
+        (1, 2, 1), (1, 0, 2), (1, 1, 2), (1, 2, 2),
     ),
 }
-STEPS = 4
-FIRST = 4 * LAYERS
+SLOTS = tuple(
+    (chunk, part, step)
+    for chunk in range(CHUNKS)
+    for part in range(len(ORDERS[chunk]))
+    for step in range(len(LABELS[chunk]))
+)
+FIRST = 8 * LAYERS
 LATER = FIRST + CHUNKS
-LOSS = LATER + CHUNKS * len(ORDERS) * STEPS
-COPIES = LOSS + STEPS + 1
+LOSS = LATER + len(SLOTS)
+COPIES = LOSS + 5
 
 
 def smooth_slope(values):
@@ -174,8 +188,8 @@
     trunk, conv_hbm, head_hbm, targets_hbm, mask, upweight, loss_out, conv_out, head_out, trunk_out, *scratch
 ):
     conv_w, head_w, counts, local_sem, send_sem, recv_sem, acts, grads, streams, slopes = scratch[:10]
-    stream_grad, weights, sums, turned = scratch[10:14]
-    scratch = scratch[3:]
+    stream_grad, weights, sums, turned, other_acts, other_grads = scratch[10:16]
+    scratch = scratch[5:]
     terms, first, later, loss_slots = (
         scratch[11 : 11 + CHUNKS],
         scratch[11 + CHUNKS : 11 + 2 * CHUNKS],
@@ -247,9 +261,8 @@
         )
         return up, down
 
-    def send_edges(buffer, layer, number, block):
+    def send_edges(buffer, layer, number):
         spread, start = spreads[layer], starts[layer]
-        buffer[pl.ds(start + spread, rows)] = block
         up, down = edges(buffer, layer, number)
 
         @pl.when(has_right)
@@ -284,17 +297,43 @@
     def view(buffer, layer, tap):
         return buffer[pl.ds(starts[layer] + tap * spreads[layer], rows)]
 
+    side = channels // 2
+    my_side = pl.ds(pl.multiple_of(samp * side, 128), side)
+    other_side = pl.ds(pl.multiple_of((1 - samp) * side, 128), side)
+
+    def middle_rows(layer):
+        return pl.ds(starts[layer] + spreads[layer], rows)
+
+    def act_copy(layer):
+        place_of = middle_rows(layer)
+        return remote(
+            acts.at[place_of], other_acts.at[place_of], 8 * layer + 6, partner["samp"]
+        )
+
+    def grad_copy(layer):
+        return remote(
+            grads.at[middle_rows(layer), other_side],
+            other_grads.at[layer],
+            8 * layer + 7,
+            partner["samp"],
+        )
+
     for layer in range(LAYERS):
         block = first_act
         if layer > 0:
             block = smooth(streams[layer].astype(jnp.float32)).astype(jnp.bfloat16)
-        send_edges(acts, layer, 2 * layer, block)
+        acts[middle_rows(layer)] = block
+        send_edges(acts, layer, 8 * layer)
+        act_copy(layer).start()
         conv_loads[layer].wait()
         total = streams[layer].astype(jnp.float32) + dot(view(acts, layer, 1), conv_w[layer, 1], 1, 0)
-        wait_edges(acts, layer, 2 * layer)
+        wait_edges(acts, layer, 8 * layer)
         for tap in (0, 2):
             total += dot(view(acts, layer, tap), conv_w[layer, tap], 1, 0)
         streams[layer + 1] = total.astype(jnp.bfloat16)
+        if layer > 0:
+            act_copy(layer - 1).wait()
+            send_edges(other_acts, layer - 1, 8 * (layer - 1) + 2)
 
     head_load.wait()
     count_load.wait()
@@ -305,18 +344,21 @@
 
     def first_copy(chunk):
         return remote(
-            terms[chunk].at[:, :, :, :, 1 - bits[0]], first[chunk], FIRST + chunk, partner[0]
+            terms[chunk].at[(slice(None),) * len(LABELS[chunk]) + (1 - bits[0],)],
+            first[chunk],
+            FIRST + chunk,
+            partner[0],
         )
 
     def part_rows(chunk, part):
         return pl.ds(CUTS[chunk][part], CUTS[chunk][part + 1] - CUTS[chunk][part])
 
     def slot(chunk, part, step):
-        return later[(chunk * len(ORDERS) + part) * STEPS + step]
+        return later[SLOTS.index((chunk, part, step))]
 
     def picked(chunk, part, step, which):
-        order = ORDERS[part]
-        labels = ["samp", 3, 2, 1]
+        order = ORDERS[chunk][part]
+        labels = list(LABELS[chunk])
         for done in order[:step]:
             labels.remove(done)
         dim = labels.index(order[step])
@@ -331,8 +373,8 @@
             src = first[chunk].at[tuple(at) + (part_rows(chunk, part),)]
         else:
             src = slot(chunk, part, step - 1).at[tuple(at)]
-        number = LATER + (chunk * len(ORDERS) + part) * STEPS + step
-        return remote(src, slot(chunk, part, step), number, partner[ORDERS[part][step]])
+        number = LATER + SLOTS.index((chunk, part, step))
+        return remote(src, slot(chunk, part, step), number, partner[ORDERS[chunk][part][step]])
 
     def added(a, b):
         return a.astype(jnp.float32) + b.astype(jnp.float32)
@@ -344,14 +386,14 @@
         first_copy(chunk).wait()
 
         def add(number, carry):
-            at = digits(number, 4)
+            at = digits(number, len(LABELS[chunk]))
             first[chunk][at] = added(first[chunk][at], terms[chunk][at + (bits[0],)]).astype(
                 jnp.bfloat16
             )
             return carry
 
-        lax.fori_loop(0, 16, add, 0)
-        for part in range(len(ORDERS)):
+        lax.fori_loop(0, 2 ** len(LABELS[chunk]), add, 0)
+        for part in range(len(ORDERS[chunk])):
             later_copy(chunk, part, 0).start()
 
     def advance(chunk, part, step):
@@ -367,7 +409,7 @@
                 there = there + (part_rows(chunk, part),)
             return added(held[at] if at else held[...], before[there])
 
-        if step == STEPS - 1:
+        if step == len(LABELS[chunk]) - 1:
             where = part_rows(chunk, part)
             total = values(()) * factor()
             if chunk == 0:
@@ -405,13 +447,13 @@
         loss_copy(step).wait()
         sums[...] += loss_slots[2 * step + 1]
 
-    def put(chunk, value, row, side):
-        size = terms[chunk].shape[5]
+    def put(chunk, value, row):
+        size = terms[chunk].shape[4]
         at = 0
         while at < value.shape[0]:
             block, inner = divmod(row + at, size)
             length = min(size - inner, value.shape[0] - at)
-            where = (side,) + tuple((block >> b) & 1 for b in (3, 2, 1, 0))
+            where = tuple((block >> b) & 1 for b in (3, 2, 1, 0))
             terms[chunk][where + (pl.ds(inner, length),)] = value[at : at + length].astype(jnp.bfloat16)
             at += length
 
@@ -448,37 +490,47 @@
     loss_start(0)
     stream_grad[...] = dot(slopes[...], head_w[...], 1, 1)
 
+    def send_grad(layer):
+        grads[middle_rows(layer)] = stream_grad[...].astype(jnp.bfloat16)
+        send_edges(grads, layer, 8 * layer + 4)
+        grad_copy(layer).start()
+
     def begin_and_turn(chunk):
         start_later(chunk)
         for turn in TURNS[chunk]:
             advance(*turn)
 
+    send_grad(LAYERS - 1)
+    act_copy(LAYERS - 1).wait()
+    send_edges(other_acts, LAYERS - 1, 8 * (LAYERS - 1) + 2)
     chunk = 0
     for layer in reversed(range(LAYERS)):
-        number = 2 * LAYERS + 2 * layer
-        send_edges(grads, layer, number, stream_grad[...].astype(jnp.bfloat16))
-        middle = view(grads, layer, 1)
-        for tap in range(3):
-            for begin in range(0, channels, 384):
-                seen = acts[pl.ds(starts[layer] + tap * spreads[layer], rows), begin : begin + 384]
-                value = dot(seen, middle, 0, 0)
-                for side in range(2):
-                    put(
-                        layer + 1,
-                        value[:, side * channels // 2 : (side + 1) * channels // 2],
-                        tap * channels + begin,
-                        side,
-                    )
-        first_copy(layer + 1).start()
+        total = dot(view(grads, layer, 1), conv_w[layer, 1], 1, 1)
         begin_and_turn(chunk)
         chunk = layer + 1
-        loss_end(LAYERS - 1 - layer)
-        loss_start(LAYERS - layer)
-        total = dot(middle, conv_w[layer, 1], 1, 1)
-        wait_edges(grads, layer, number)
+        wait_edges(grads, layer, 8 * layer + 4)
         for tap in (0, 2):
             total += dot(view(grads, layer, 2 - tap), conv_w[layer, tap], 1, 1)
         stream_grad[...] += smooth_slope(streams[layer].astype(jnp.float32)) * total
+        if layer > 0:
+            send_grad(layer - 1)
+        loss_end(LAYERS - 1 - layer)
+        loss_start(LAYERS - layer)
+        wait_edges(other_acts, layer, 8 * layer + 2)
+        grad_copy(layer).wait()
+        both = jnp.concatenate([grads[middle_rows(layer), my_side], other_grads[layer]], axis=0)
+        for tap in range(3):
+            place_of = pl.ds(starts[layer] + tap * spreads[layer], rows)
+            for begin in range(0, channels, 384):
+                seen = jnp.concatenate(
+                    [
+                        acts[place_of, begin : begin + 384],
+                        other_acts[place_of, begin : begin + 384],
+                    ],
+                    axis=0,
+                )
+                put(layer + 1, dot(seen, both, 0, 0), tap * channels + begin)
+        first_copy(layer + 1).start()
     loss_end(3)
     loss_start(4)
     start_later(1)
@@ -516,14 +568,16 @@
         pltpu.VMEM((rows, 128), jnp.float32),
         pltpu.VMEM((16, 128), jnp.float32),
         vmem((channels, rows)),
+        vmem((extended_rows, channels)),
+        vmem((LAYERS, rows, channels // 2)),
     ]
-    scratch += [vmem((2,) * 5 + size) for size in sizes]
-    scratch += [vmem((2,) * 4 + size) for size in sizes]
-    for size, cut in zip(sizes, CUTS):
-        for part in range(len(ORDERS)):
-            for step in range(STEPS):
-                scratch.append(vmem((2,) * (3 - step) + (cut[part + 1] - cut[part], size[1])))
-    scratch.append(pltpu.VMEM((2 * (STEPS + 1), 16, 128), jnp.float32))
+    counts = [len(labels) for labels in LABELS]
+    scratch += [vmem((2,) * (count + 1) + size) for count, size in zip(counts, sizes)]
+    scratch += [vmem((2,) * count + size) for count, size in zip(counts, sizes)]
+    for chunk, part, step in SLOTS:
+        part_rows = CUTS[chunk][part + 1] - CUTS[chunk][part]
+        scratch.append(vmem((2,) * (counts[chunk] - 1 - step) + (part_rows, sizes[chunk][1])))
+    scratch.append(pltpu.VMEM((10, 16, 128), jnp.float32))
     whole = pl.BlockSpec(memory_space=pltpu.VMEM)
     away = pl.BlockSpec(memory_space=pl.ANY)
     loss, conv_grad, head_grad, trunk_grad = pl.pallas_call(

time: 129 us -> 122 us (0.946)
  Pallas kernels: 121 us -> 114 us
    pallas_call x1, Pallas kernels: 121 us -> 114 us  [per_device_kernel(): pl.pallas_call(kernel, out_shape=(jax.ShapeDtypeStruct((1, 1), jnp.float3...]
where the time goes in v4:
time: 122 us
  Pallas kernels  114 us (93%)
  local copies, waits for them, and re-layouts  5.41 us (4%)
  between operations  2.34 us (2%)
    pallas_call x1, Pallas kernels, per_device_kernel(): pl.pallas_call(kernel, out_shape=(jax.ShapeDtypeStruct((1, 1), jnp.float3...  114 us
    unnamed x3, local copies, waits for them, and re-layouts  5.41 us

profile of v4, /device:TPU:0, one launch (start us, length us, event | category | flops | bytes accessed | tf_op | source)
XLA Modules:
  0.0 122.0 jit_solution(9543463701851418564)
XLA Ops:
  0.6 114.3 %shard_map.93 = (f32[1,1]{1,0:T(1,128)}, f32[3,144,384]{2,1,0:T(8,128)}, f32[48,1344]{1,0:T(8,128)}, bf16[256,768]{1,0:T(8,128)(2,1)}) custom-call(bf16[256,768]{1,0:T(8,128)(2,1)} %bitcast.6, bf16[3,3,768,768]{3,2,1,0:T(8,128)(2,1)} %conv_hbm.1, bf16[768,2688]{1,0:T(8,128)(2,1)} %head_hbm.1, s32[256,2688]{1,0:T(8,128)} %bitcast.4, s32[1,256]{1,0:T(1,128)} %mask.1, ...), custom_call_target="tpu_custom_call" | custom-call | tf_op jit(solution)/shard_map/pallas_call | solution.py:583
  115.5 2.0 %copy.15 = f32[3,144,384]{2,1,0:T(8,128)} copy(f32[3,144,384]{2,1,0:T(8,128)} %get-tuple-element.17) | data formatting | bytes 1327104
  117.4 1.7 %copy.16 = f32[48,1344]{1,0:T(8,128)} copy(f32[48,1344]{1,0:T(8,128)} %get-tuple-element.18) | data formatting | bytes 516096
  119.1 1.8 %copy.17 = bf16[1,256,768]{2,1,0:T(8,128)(2,1)} copy(bf16[1,256,768]{2,1,0:T(8,128)(2,1)} %bitcast.5) | data formatting | bytes 786432

commit v5 on v4

--- a/solution.py
+++ b/solution.py
@@ -134,12 +134,12 @@
 TILE = 384
 ORDERS = (
     (("samp", 1, 2, 3), (1, "samp", 2, 3), (2, 3, "samp", 1)),
-    ((1, 2, 3), (1, 2, 3), (1, 2, 3)),
+    ((1, 2, 3), (1, 2, 3)),
     ((1, 2, 3), (2, 3, 1)),
     ((1, 2, 3), (2, 3, 1)),
 )
 LABELS = (("samp", 3, 2, 1), (3, 2, 1), (3, 2, 1), (3, 2, 1))
-CUTS = ((0, 16, 32, 48), (0, 48, 96, 144), (0, 128, 144), (0, 80, 144))
+CUTS = ((0, 16, 32, 48), (0, 80, 144), (0, 80, 144), (0, 64, 144))
 CHUNKS = LAYERS + 1
 TURNS = {
     0: (
@@ -147,14 +147,14 @@
     3: (
     ),
     2: (
-        (0, 0, 0), (0, 1, 0), (0, 2, 0), (3, 1, 0), (3, 0, 0),
+        (0, 2, 0), (0, 0, 0), (0, 1, 0), (3, 1, 0),
     ),
     1: (
-        (2, 1, 0), (0, 1, 1), (0, 2, 1), (3, 1, 1), (2, 0, 0), (3, 0, 1),
-        (2, 1, 1), (0, 2, 2), (0, 0, 1), (0, 1, 2), (1, 0, 0), (2, 0, 1),
-        (3, 0, 2), (1, 1, 0), (0, 0, 2), (0, 1, 3), (1, 2, 0), (1, 0, 1),
-        (3, 1, 2), (2, 1, 2), (0, 2, 3), (2, 0, 2), (1, 1, 1), (0, 0, 3),
-        (1, 2, 1), (1, 0, 2), (1, 1, 2), (1, 2, 2),
+        (3, 0, 0), (2, 1, 0), (2, 0, 0), (0, 1, 1), (0, 2, 1), (3, 1, 1),
+        (0, 0, 1), (3, 0, 1), (0, 2, 2), (2, 1, 1), (1, 0, 0), (2, 0, 1),
+        (0, 1, 2), (1, 1, 0), (0, 0, 2), (3, 1, 2), (3, 0, 2), (0, 2, 3),
+        (2, 1, 2), (1, 0, 1), (2, 0, 2), (0, 1, 3), (1, 1, 1), (0, 0, 3),
+        (1, 0, 2), (1, 1, 2),
     ),
 }
 SLOTS = tuple(
@@ -331,9 +331,10 @@
         for tap in (0, 2):
             total += dot(view(acts, layer, tap), conv_w[layer, tap], 1, 0)
         streams[layer + 1] = total.astype(jnp.bfloat16)
-        if layer > 0:
-            act_copy(layer - 1).wait()
-            send_edges(other_acts, layer - 1, 8 * (layer - 1) + 2)
+
+    for layer in reversed(range(LAYERS)):
+        act_copy(layer).wait()
+        send_edges(other_acts, layer, 8 * layer + 2)
 
     head_load.wait()
     count_load.wait()
@@ -492,8 +493,8 @@
 
     def send_grad(layer):
         grads[middle_rows(layer)] = stream_grad[...].astype(jnp.bfloat16)
+        grad_copy(layer).start()
         send_edges(grads, layer, 8 * layer + 4)
-        grad_copy(layer).start()
 
     def begin_and_turn(chunk):
         start_later(chunk)
@@ -501,21 +502,11 @@
             advance(*turn)
 
     send_grad(LAYERS - 1)
-    act_copy(LAYERS - 1).wait()
-    send_edges(other_acts, LAYERS - 1, 8 * (LAYERS - 1) + 2)
     chunk = 0
     for layer in reversed(range(LAYERS)):
-        total = dot(view(grads, layer, 1), conv_w[layer, 1], 1, 1)
         begin_and_turn(chunk)
         chunk = layer + 1
-        wait_edges(grads, layer, 8 * layer + 4)
-        for tap in (0, 2):
-            total += dot(view(grads, layer, 2 - tap), conv_w[layer, tap], 1, 1)
-        stream_grad[...] += smooth_slope(streams[layer].astype(jnp.float32)) * total
-        if layer > 0:
-            send_grad(layer - 1)
-        loss_end(LAYERS - 1 - layer)
-        loss_start(LAYERS - layer)
+        total = dot(view(grads, layer, 1), conv_w[layer, 1], 1, 1)
         wait_edges(other_acts, layer, 8 * layer + 2)
         grad_copy(layer).wait()
         both = jnp.concatenate([grads[middle_rows(layer), my_side], other_grads[layer]], axis=0)
@@ -531,6 +522,14 @@
                 )
                 put(layer + 1, dot(seen, both, 0, 0), tap * channels + begin)
         first_copy(layer + 1).start()
+        loss_end(LAYERS - 1 - layer)
+        loss_start(LAYERS - layer)
+        wait_edges(grads, layer, 8 * layer + 4)
+        for tap in (0, 2):
+            total += dot(view(grads, layer, 2 - tap), conv_w[layer, tap], 1, 1)
+        stream_grad[...] += smooth_slope(streams[layer].astype(jnp.float32)) * total
+        if layer > 0:
+            send_grad(layer - 1)
     loss_end(3)
     loss_start(4)
     start_later(1)
@@ -541,6 +540,17 @@
     ) / (OUTPUT_TRACKS * weight_sum())
     for turn in TURNS[1]:
         advance(*turn)
+
+
+def settle(*refs):
+    sources, targets, sems = refs[:3], refs[3:6], refs[6]
+    copies = [
+        pltpu.make_async_copy(a, b, sems.at[i]) for i, (a, b) in enumerate(zip(sources, targets))
+    ]
+    for copy in copies:
+        copy.start()
+    for copy in copies:
+        copy.wait()
 
 
 def per_device_kernel(trunk, conv_weight, head_weight, targets, error_mask, upweight):
@@ -602,6 +612,15 @@
         error_mask,
         upweight,
     )
+    results = (conv_grad, head_grad, trunk_grad)
+    conv_grad, head_grad, trunk_grad = pl.pallas_call(
+        settle,
+        out_shape=tuple(jax.ShapeDtypeStruct(r.shape, r.dtype) for r in results),
+        in_specs=[away] * 3,
+        out_specs=(away,) * 3,
+        scratch_shapes=[pltpu.SemaphoreType.DMA((3,))],
+        compiler_params=pltpu.CompilerParams(vmem_limit_bytes=63 * 2**20),
+    )(*results)
     return loss.reshape(()), conv_grad, head_grad, trunk_grad.reshape(trunk.shape)
 
 

time: 122 us -> 163 us (1.34)
  Pallas kernels: 114 us -> 160 us
  local copies, waits for them, and re-layouts: 5.41 us -> 0 us
    pallas_call x0 -> x1, Pallas kernels: none -> 41.3 us  [per_device_kernel(): pl.pallas_call(settle, out_shape=tuple((jax.ShapeDtypeStruct(r.shape, r.d...]
    unnamed x3 -> x0, local copies, waits for them, and re-layouts: 5.41 us -> none
    pallas_call x1, Pallas kernels: 114 us -> 119 us  [per_device_kernel(): pl.pallas_call(kernel, out_shape=(jax.ShapeDtypeStruct((1, 1), jnp.float3...]
where the time goes in v5:
time: 163 us; the launch traced here: 162 us
  Pallas kernels  160 us (98%)
  between operations  2.41 us (1%)
    pallas_call x1, Pallas kernels, per_device_kernel(): pl.pallas_call(kernel, out_shape=(jax.ShapeDtypeStruct((1, 1), jnp.float3...  119 us
    pallas_call x1, Pallas kernels, per_device_kernel(): pl.pallas_call(settle, out_shape=tuple((jax.ShapeDtypeStruct(r.shape, r.d...  41.3 us

profile of v5, /device:TPU:0, one launch (start us, length us, event | category | flops | bytes accessed | tf_op | source)
XLA Modules:
  0.0 162.4 jit_solution(11561522661293299503)
XLA Ops:
  0.6 118.7 %shard_map.93 = (f32[1,1]{1,0:T(1,128)}, f32[3,144,384]{2,1,0:T(8,128)}, f32[48,1344]{1,0:T(8,128)}, bf16[256,768]{1,0:T(8,128)(2,1)}) custom-call(bf16[256,768]{1,0:T(8,128)(2,1)} %bitcast.5, bf16[3,3,768,768]{3,2,1,0:T(8,128)(2,1)} %conv_hbm.1, bf16[768,2688]{1,0:T(8,128)(2,1)} %head_hbm.1, s32[256,2688]{1,0:T(8,128)} %bitcast.4, s32[1,256]{1,0:T(1,128)} %mask.1, ...), custom_call_target="tpu_custom_call" | custom-call | tf_op jit(solution)/shard_map/pallas_call | solution.py:593
  119.3 41.3 %shard_map.94 = (f32[3,144,384]{2,1,0:T(8,128)}, f32[48,1344]{1,0:T(8,128)}, bf16[256,768]{1,0:T(8,128)(2,1)}) custom-call(f32[3,144,384]{2,1,0:T(8,128)} %get-tuple-element.12.refs_0_, f32[48,1344]{1,0:T(8,128)} %get-tuple-element.13.refs_1_, bf16[256,768]{1,0:T(8,128)(2,1)} %get-tuple-element.14.refs_2_), custom_call_target="tpu_custom_call" | custom-call | tf_op jit(solution)/shard_map/pallas_call | solution.py:616

commit v6 on v4

--- a/solution.py
+++ b/solution.py
@@ -331,9 +331,10 @@
         for tap in (0, 2):
             total += dot(view(acts, layer, tap), conv_w[layer, tap], 1, 0)
         streams[layer + 1] = total.astype(jnp.bfloat16)
-        if layer > 0:
-            act_copy(layer - 1).wait()
-            send_edges(other_acts, layer - 1, 8 * (layer - 1) + 2)
+
+    for layer in reversed(range(LAYERS)):
+        act_copy(layer).wait()
+        send_edges(other_acts, layer, 8 * layer + 2)
 
     head_load.wait()
     count_load.wait()
@@ -501,8 +502,6 @@
             advance(*turn)
 
     send_grad(LAYERS - 1)
-    act_copy(LAYERS - 1).wait()
-    send_edges(other_acts, LAYERS - 1, 8 * (LAYERS - 1) + 2)
     chunk = 0
     for layer in reversed(range(LAYERS)):
         total = dot(view(grads, layer, 1), conv_w[layer, 1], 1, 1)

time: 122 us -> 126 us (1.033)
  Pallas kernels: 114 us -> 118 us
    pallas_call x1, Pallas kernels: 114 us -> 118 us  [per_device_kernel(): pl.pallas_call(kernel, out_shape=(jax.ShapeDtypeStruct((1, 1), jnp.float3...]
where the time goes in v6:
time: 126 us
  Pallas kernels  118 us (94%)
  local copies, waits for them, and re-layouts  5.41 us (4%)
  between operations  2.34 us (2%)
    pallas_call x1, Pallas kernels, per_device_kernel(): pl.pallas_call(kernel, out_shape=(jax.ShapeDtypeStruct((1, 1), jnp.float3...  118 us
    unnamed x3, local copies, waits for them, and re-layouts  5.41 us

profile of v6, /device:TPU:0, one launch (start us, length us, event | category | flops | bytes accessed | tf_op | source)
XLA Modules:
  0.0 126.0 jit_solution(13474689590515813723)
XLA Ops:
  0.6 118.2 %shard_map.93 = (f32[1,1]{1,0:T(1,128)}, f32[3,144,384]{2,1,0:T(8,128)}, f32[48,1344]{1,0:T(8,128)}, bf16[256,768]{1,0:T(8,128)(2,1)}) custom-call(bf16[256,768]{1,0:T(8,128)(2,1)} %bitcast.6, bf16[3,3,768,768]{3,2,1,0:T(8,128)(2,1)} %conv_hbm.1, bf16[768,2688]{1,0:T(8,128)(2,1)} %head_hbm.1, s32[256,2688]{1,0:T(8,128)} %bitcast.4, s32[1,256]{1,0:T(1,128)} %mask.1, ...), custom_call_target="tpu_custom_call" | custom-call | tf_op jit(solution)/shard_map/pallas_call | solution.py:582
  119.4 2.0 %copy.15 = f32[3,144,384]{2,1,0:T(8,128)} copy(f32[3,144,384]{2,1,0:T(8,128)} %get-tuple-element.17) | data formatting | bytes 1327104
  121.4 1.7 %copy.16 = f32[48,1344]{1,0:T(8,128)} copy(f32[48,1344]{1,0:T(8,128)} %get-tuple-element.18) | data formatting | bytes 516096
  123.1 1.8 %copy.17 = bf16[1,256,768]{2,1,0:T(8,128)(2,1)} copy(bf16[1,256,768]{2,1,0:T(8,128)(2,1)} %bitcast.5) | data formatting | bytes 786432
